TPU v7x, 1024 devices: a whole 4x4x32 slice. The times are simulated.
1024 devices in a mesh: dp: 128 (over y, z), tensor: 8 (over x, core).
Axes of the slice: x: 4, y: 4, z: 32, core: 2. Of those that a mesh axis runs over, the one named last changes fastest.
Arguments:
- gradient: bfloat16 [56, 512, 512], P(None, 'dp', 'tensor'), may hold values from -100 to 100
- second_moment: float32 [56, 512, 512], P(None, 'dp', 'tensor'), may hold values from 0 to 64
- factors: bfloat16 [56, 2, 512, 512], P(None, None, 'dp', 'tensor'), may hold values from -2 to 2, as said below
- old_owner: int32 [56], replicated, may hold values from 0 to 127, as said below
- new_owner: int32 [56], replicated, may hold values from 0 to 127, as said below
- offsets: int32 [56], replicated, may hold values from 0 to 55, each once
Outputs:
- direction: bfloat16 [56, 512, 512], P(None, 'dp', 'tensor')
- moment_new: float32 [56, 512, 512], P(None, 'dp', 'tensor')
- owner_grafts: float32 [128, 2], P('dp')
Inputs may be any that keep to these rules, and one draw needn't show every extreme that they name: `old_owner`: each device of dp owned at most 2 blocks, and one owned exactly 2. `new_owner`: each device of dp owns at most 2 blocks, and one owns exactly 2. Every block factors[s, i] is symmetric.
All inputs are finite; a program needn't handle non-finite values.
Results may differ from a plain program's by a relative error of at most 0.0057.
Values may be sent and summed in bfloat16 or wider, within the bound.
No kernel may reach another device: no remote copies, remote signals or barrier semaphores. Data moves between devices by JAX's collectives and lax.ppermute only.
A program may use at most 64 MiB of HBM per device.

v0:
```python
import jax
import jax.numpy as jnp
from jax import lax
from jax.sharding import PartitionSpec as P

BETA_TWO = 0.99
ADAM_EPS = 1e-08
NORM_EPS = 1e-06


def checkpoint_slots(old_owner):
    positions = jnp.arange(old_owner.shape[0], dtype=jnp.int32)
    before = old_owner[None, :] < old_owner[:, None]
    tied_before = (old_owner[None, :] == old_owner[:, None]) & (
        positions[None, :] < positions[:, None]
    )
    return jnp.sum((before | tied_before).astype(jnp.int32), axis=1)


def owner_ranks(new_owner):
    positions = jnp.arange(new_owner.shape[0], dtype=jnp.int32)
    tied_before = (new_owner[None, :] == new_owner[:, None]) & (
        positions[None, :] < positions[:, None]
    )
    return jnp.sum(tied_before.astype(jnp.int32), axis=1)


def route_pieces(pieces, owners, rank_list, dp_count, capacity):
    buffer = jnp.zeros((dp_count, capacity) + pieces.shape[1:], pieces.dtype)
    return buffer.at[owners, rank_list].set(pieces)


def per_device(gradient, second_moment, factors, old_owner, new_owner, offsets):
    dp_count = lax.axis_size("dp")
    myself = lax.axis_index("dp")
    blocks = gradient.shape[0]
    capacity = max(2, 2 * blocks // dp_count)
    wide_grad = gradient.astype(jnp.float32)
    moment_new = BETA_TWO * second_moment + (1.0 - BETA_TWO) * wide_grad * wide_grad
    adam_step = wide_grad / (jnp.sqrt(moment_new) + ADAM_EPS)
    adam_sq = jnp.sum(adam_step * adam_step, axis=(1, 2))
    owner_rank = owner_ranks(new_owner)
    ckpt_slots = checkpoint_slots(old_owner)
    positions = jnp.arange(blocks, dtype=jnp.int32)
    matches = (new_owner[:, None] == myself) & (
        owner_rank[:, None] == jnp.arange(capacity, dtype=jnp.int32)[None, :]
    )
    held_block = jnp.sum(jnp.where(matches, positions[:, None], 0), axis=0)
    held_valid = jnp.any(matches, axis=0)
    outgoing = route_pieces(
        jnp.swapaxes(gradient[offsets], 1, 2), new_owner, owner_rank, dp_count, capacity
    )
    arrived = lax.all_to_all(outgoing, "dp", split_axis=0, concat_axis=3, tiled=True)
    grad_rows = arrived[0]
    wanted = ckpt_slots[held_block]
    chosen = jnp.swapaxes(lax.all_gather(factors, "dp", axis=2, tiled=True)[wanted], 2, 3)
    left_rows = chosen[:, 0]
    right_rows = chosen[:, 1]
    left_full, grad_full = (
        lax.all_gather(left_rows, "tensor", axis=1, tiled=True),
        lax.all_gather(grad_rows, "tensor", axis=1, tiled=True),
    )
    product = jnp.einsum(
        "sik,skj->sij", right_rows, grad_full, preferred_element_type=jnp.float32
    ).astype(jnp.bfloat16)
    transposed = jnp.einsum(
        "sij,sjr->sir", product, left_full, preferred_element_type=jnp.float32
    ).astype(jnp.bfloat16)
    cols_here = transposed.shape[1]
    block_len = transposed.shape[2]
    returning = jnp.transpose(
        transposed.reshape(capacity, cols_here, dp_count, block_len // dp_count), (2, 0, 3, 1)
    )
    returned = lax.all_to_all(returning, "dp", split_axis=0, concat_axis=0, tiled=True)
    pieces_back = returned[new_owner, owner_rank]
    wide_back = pieces_back.astype(jnp.float32)
    adam_total, shampoo_total = lax.psum(
        (adam_sq[offsets], jnp.sum(wide_back * wide_back, axis=(1, 2))), ("dp", "tensor")
    )
    graft_scale = jnp.sqrt(adam_total / (shampoo_total + NORM_EPS))
    block_dir = (graft_scale[:, None, None] * wide_back).astype(jnp.bfloat16)
    own_grafts = jnp.where(held_valid, graft_scale[held_block], 0.0)
    direction = jnp.zeros(gradient.shape, jnp.bfloat16).at[offsets].set(block_dir)
    return (direction, moment_new, own_grafts[None, :])


def solution(mesh):
    placed = (
        P(None, "dp", "tensor"),
        P(None, "dp", "tensor"),
        P(None, None, "dp", "tensor"),
        P(),
        P(),
        P(),
    )
    return jax.shard_map(
        per_device,
        mesh=mesh,
        in_specs=placed,
        out_specs=(P(None, "dp", "tensor"), P(None, "dp", "tensor"), P("dp", None)),
        check_vma=False,
    )
```

profile of v0, /device:TPU:1, one launch (start us, length us, event | category | flops | bytes accessed | tf_op | source)
XLA Modules:
  0.0 631.1 jit_solution(8165809815631232553)
XLA Ops:
  7.2 1.6 copy.22
  8.8 0.7 compare_select_fusion.4
  9.5 1.5 gather_fusion.3
  11.0 0.9 convert_reduce_fusion
  11.9 0.7 fusion.18
  12.6 3.2 scatter_fusion
  15.8 0.2 reshape.135
  16.0 66.4 %all_to_all.20 = bf16[128,2,256]{2,1,0:T(2,128)(2,1)S(1)} all-to-all(bf16[128,2,256]{2,1,0:T(2,128)(2,1)S(1)} %reshape.135), channel_id=1, replica_groups=mesh['dp'=128,'tensor'=8] {'dp'}, dimensions={0} | all-to-all | bytes 262144 | tf_op jit(solution)/shard_map/all_to_all | solution.py:53
  82.5 0.2 reshape.136
  82.9 0.8 copy.26
  83.8 0.7 broadcast_compare_fusion
  84.6 0.9 convert_reduce_fusion.1
  85.5 0.6 gather_fusion.1
  86.2 225.0 %all-gather.5.cloned.1.call-done = bf16[56,2,512,64]{3,0,1,2:T(8,128)(2,1)} async-done(((bf16[56,2,4,64]{3,0,1,2:T(8,128)(2,1)}), bf16[56,2,512,64]{3,0,1,2:T(8,128)(2,1)}) %all-gather.5.cloned.1.call-update) | async-done | bytes 7340048 | tf_op jit(solution)/shard_map/all_gather | solution.py:56
  311.1 16.2 %copy.23 = bf16[56,2,512,64]{2,3,1,0:T(8,128)(2,1)} copy(bf16[56,2,512,64]{3,0,1,2:T(8,128)(2,1)} %all-gather.5.cloned.1.call-done) | data formatting | bytes 14680064 | tf_op jit(solution)/shard_map/all_gather | solution.py:56
  327.3 3.6 gather_fusion.2
  331.0 0.7 slice.23
  331.6 30.7 %all-gather.7.cloned.1.call-done = bf16[2,512,512]{2,0,1:T(2,128)(2,1)} async-done(((bf16[2,64,512]{2,0,1:T(2,128)(2,1)}), bf16[2,512,512]{2,0,1:T(2,128)(2,1)}) %all-gather.7.cloned.1.call-update) | async-done | bytes 1048592 | tf_op jit(solution)/shard_map/all_gather | solution.py:61
  362.4 44.1 %all-gather.9.cloned.1.call-done = bf16[2,1,512,512]{3,2,0,1:T(8,128)(2,1)} async-done(((bf16[2,1,64,512]{3,2,0,1:T(8,128)(2,1)}), bf16[2,1,512,512]{3,2,0,1:T(8,128)(2,1)}) %all-gather.9.cloned.1.call-update) | async-done | bytes 1048592 | tf_op jit(solution)/shard_map/all_gather | solution.py:60
  406.4 2.0 convolution_convert_fusion
  408.7 0.9 reshape.137
  409.6 26.8 %all-to-all-start.1 = ((bf16[128,2,256]{2,1,0:T(2,128)(2,1)}), bf16[128,2,256]{2,1,0:T(2,128)(2,1)S(1)}, u32[]{:S(2)}, u32[]{:S(2)}) async-start(bf16[128,2,256]{2,1,0:T(2,128)(2,1)} %reshape.137), calls=%async_computation.1 | async-start | bytes 262144 | tf_op jit(solution)/shard_map/all_to_all | solution.py:74
  436.4 0.9 fusion.7
  437.3 0.8 gather_fusion
  438.2 29.4 %all-to-all-done.1 = bf16[128,2,256]{2,1,0:T(2,128)(2,1)S(1)} async-done(((bf16[128,2,256]{2,1,0:T(2,128)(2,1)}), bf16[128,2,256]{2,1,0:T(2,128)(2,1)S(1)}, u32[]{:S(2)}, u32[]{:S(2)}) %all-to-all-start.1) | async-done | bytes 131104 | tf_op jit(solution)/shard_map/all_to_all | solution.py:74
  467.6 0.2 reshape.138
  467.8 0.9 gather_fusion.4
  468.7 0.5 fusion.4
  469.2 151.4 %all-reduce = (f32[56]{0:T(128)S(1)}, f32[56]{0:T(128)S(1)}) all-reduce(f32[56]{0:T(128)S(1)} %gather_fusion, f32[56]{0:T(128)S(1)} %fusion.4), channel_id=1, replica_groups=mesh['dp'=128,'tensor'=8] {'dp','tensor'}, use_global_device_ids=true, to_apply=%region_1.0 | all-reduce | flops 112 | bytes 896 | tf_op jit(solution)/shard_map/psum | solution.py:77
  620.8 0.6 gather_fusion.5
  621.4 2.5 scatter_fusion.1
  623.9 0.5 select_bitcast_fusion
  (28 shorter events, 1.3 us)
Async XLA Ops:
  7.2 303.9 %all-gather.5.cloned.1.call-start = ((), (), s32[]{:S(2)}) async-start(), calls=%async_computation.2 | async-start | bytes 14794752 | tf_op jit(solution)/shard_map/all_gather | solution.py:56
  8.8 353.6 %all-gather.7.cloned.1.call-start = ((), (), s32[]{:S(2)}) async-start(), calls=%async_computation.3 | async-start | bytes 1179648 | tf_op jit(solution)/shard_map/all_gather | solution.py:61
  83.7 322.7 %all-gather.9.cloned.1.call-start = ((), (), s32[]{:S(2)}) async-start(), calls=%async_computation.4 | async-start | bytes 1179648 | tf_op jit(solution)/shard_map/all_gather | solution.py:60
  86.1 350.2 %copy-start = (bf16[56,4,64]{2,1,0:T(4,128)(2,1)S(1)}, bf16[56,4,64]{2,1,0:T(4,128)(2,1)}, u32[]{:S(2)}) copy-start(bf16[56,4,64]{2,1,0:T(4,128)(2,1)} %param.6) | copy-start | bytes 86020
  86.1 350.2 %copy-start.2 = (f32[56,4,64]{2,1,0:T(4,128)S(1)}, f32[56,4,64]{2,1,0:T(4,128)}, u32[]{:S(2)}) copy-start(f32[56,4,64]{2,1,0:T(4,128)} %param.7) | copy-start | bytes 172036
  409.6 58.0 %all-to-all-start.1 = ((bf16[128,2,256]{2,1,0:T(2,128)(2,1)}), bf16[128,2,256]{2,1,0:T(2,128)(2,1)S(1)}, u32[]{:S(2)}, u32[]{:S(2)}) async-start(bf16[128,2,256]{2,1,0:T(2,128)(2,1)} %reshape.137), calls=%async_computation.1 | async-start | bytes 262144 | tf_op jit(solution)/shard_map/all_to_all | solution.py:74
  623.9 0.6 copy-start.1
Sparse Core Ops, SparseCore 0:
  12.7 298.3 all-gather.4
  313.8 48.4 all-gather.6
  365.1 41.3 all-gather.8
where the time goes:
time: 632 us; the launch traced here: 631 us
  waiting for transfers between devices  329 us (52%)
  blocking collectives  218 us (34%)
  local copies, waits for them, and re-layouts  35.1 us (6%)
  starting transfers between devices  26.9 us (4%)
  between operations  13.9 us (2%)
    all_gather x1, waiting for transfers between devices, per_device(): lax.all_gather(factors, 'dp', axis=2, tiled=True)[wanted]  225 us
    psum x1, blocking collectives, per_device(): lax.psum((adam_sq[offsets], jnp.sum(wide_back * wide_back, axis=(1, 2))),...  151 us
    all_to_all x1, blocking collectives, per_device(): lax.all_to_all(outgoing, 'dp', split_axis=0, concat_axis=3, tiled=True)  66.4 us
    all_gather x1, waiting for transfers between devices, per_device(): lax.all_gather(left_rows, 'tensor', axis=1, tiled=True)  44.1 us
    all_gather x1, waiting for transfers between devices, per_device(): lax.all_gather(grad_rows, 'tensor', axis=1, tiled=True)  30.7 us
    all_to_all x1, waiting for transfers between devices, per_device(): lax.all_to_all(returning, 'dp', split_axis=0, concat_axis=0, tiled=True)  29.4 us
    all_to_all x1, starting transfers between devices, per_device(): lax.all_to_all(returning, 'dp', split_axis=0, concat_axis=0, tiled=True)  26.8 us
    all_gather x1, local copies, waits for them, and re-layouts, per_device(): lax.all_gather(factors, 'dp', axis=2, tiled=True)[wanted]  16.2 us
  transfers between devices with their start and end apart: 4, of which 4 were waited for; matrix products, arithmetic and copies ran while one was open for 5% of the time, Pallas kernels for 0%

commit v1 on v0

v1 whole, which is shorter than its diff:
```python
import jax
import jax.numpy as jnp
from jax import lax
from jax.experimental import pallas as pl
from jax.experimental.pallas import tpu as pltpu
from jax.sharding import Mesh
from jax.sharding import PartitionSpec as P

BETA_TWO = 0.99
ADAM_EPS = 1e-08
NORM_EPS = 1e-06
F32 = jnp.float32
BF16 = jnp.bfloat16
NB = 56
NZ = 32
VMEM = pl.BlockSpec(memory_space=pltpu.VMEM)
ANY = pl.BlockSpec(memory_space=pl.ANY)
SMEM = pl.BlockSpec(memory_space=pltpu.SMEM)


def iota(shape, dim):
    return lax.broadcasted_iota(jnp.int32, shape, dim)


def total(mask, values, axis):
    picked = jnp.where(mask, values.astype(F32), 0.0)
    return jnp.sum(picked, axis=axis, keepdims=True).astype(jnp.int32)


def one_hot(mask):
    return jnp.where(mask, 1.0, 0.0).astype(BF16)


def pick(mask, rows):
    return jnp.dot(one_hot(mask), rows, preferred_element_type=F32)


def to_column(row):
    sub, lane = iota((NB, NB), 0), iota((NB, NB), 1)
    return total(sub == lane, jnp.broadcast_to(row, (NB, NB)), 1)


def tied_before(row, column):
    sub, lane = iota((NB, NB), 0), iota((NB, NB), 1)
    return total((column == row) & (sub < lane), jnp.ones((NB, NB), jnp.int32), 0)


def slots_row(row, column):
    sub, lane = iota((NB, NB), 0), iota((NB, NB), 1)
    before = (column < row) | ((column == row) & (sub < lane))
    return total(before, jnp.ones((NB, NB), jnp.int32), 0)


def split_three(x):
    high = x.astype(BF16).astype(F32)
    rest = x - high
    mid = rest.astype(BF16).astype(F32)
    return high, mid, (rest - mid).astype(BF16).astype(F32)


def pack_kernel(
    coord_ref, grad_hbm, moment_hbm, factor_hbm, old_hbm, own_hbm, off_hbm,
    new_ref, send_ref, table_ref,
    grad_ref, moment_ref, factor_ref, old_ref, own_ref, off_ref, sems,
):
    pairs = (
        (old_hbm, old_ref),
        (off_hbm, off_ref),
        (own_hbm, own_ref),
        (grad_hbm, grad_ref),
        (moment_hbm, moment_ref),
        (factor_hbm, factor_ref),
    )
    copies = [pltpu.make_async_copy(src, dst, sems.at[i]) for i, (src, dst) in enumerate(pairs)]
    for copy in copies:
        copy.start()
    for copy in copies[:3]:
        copy.wait()
    old, own = old_ref[...], own_ref[...]
    slot = slots_row(old, to_column(old))
    slot_col, off_col = to_column(slot), to_column(off_ref[...])
    lane56 = iota((NB, NB), 1)
    position = total(slot_col == lane56, jnp.broadcast_to(off_col, (NB, NB)), 0)
    at = total(off_col == lane56, jnp.broadcast_to(slot_col, (NB, NB)), 0)
    rank = tied_before(own, to_column(own))
    held = own == coord_ref[0]
    first_row = ((slot & 1) * NZ + (slot >> 1)) * 4
    table_ref[0:1, 0:NB] = at
    for k in range(2):
        table_ref[k + 1 : k + 2, 0:NB] = jnp.where(held & (rank == k), first_row, -1)
    rows = 8 * NB
    row = iota((rows, NB), 0)
    spread = total(
        iota((rows, NB), 1) == (row >> 3), jnp.broadcast_to(position, (rows, NB)), 1
    )
    r = iota((rows, 1), 0) & 7
    source = spread * 4 + (r & 3) + 4 * NB * (r >> 2)
    for copy in copies[3:]:
        copy.wait()
    grad = grad_ref[...]
    wide = grad.astype(F32)
    moment = BETA_TWO * moment_ref[...] + (1.0 - BETA_TWO) * wide * wide
    new_ref[...] = moment
    step = wide / (jnp.sqrt(moment) + ADAM_EPS)
    high, mid, low = split_three(jnp.sum(step * step, axis=1, keepdims=True))
    lane = iota((4 * NB, 64), 1)
    sums = jnp.where(lane == 0, high, jnp.where(lane == 1, mid, jnp.where(lane == 2, low, 0.0)))
    stacked = jnp.concatenate([grad, sums.astype(BF16)], axis=0)
    mine = pick(iota((rows, rows), 1) == source, stacked).astype(BF16)
    send_ref[0:rows, :] = jnp.concatenate([factor_ref[...], mine], axis=1)
    send_ref[rows:, :] = jnp.zeros((16 * NZ - rows, 128), BF16)


def three_lanes(x, shape, first):
    lane = iota(shape, 1) - first
    high, mid, low = split_three(x)
    return jnp.where(lane == 0, high, jnp.where(lane == 1, mid, jnp.where(lane == 2, low, 0.0)))


def whole_sum(x):
    return jnp.sum(jnp.sum(x, axis=0, keepdims=True), axis=1, keepdims=True)


def spread_kernel(in_ref, out_ref):
    n = 16 * NZ
    got = in_ref[...]
    o, k = iota((256, n), 0), iota((256, n), 1)
    pairs = pick(k == ((o >> 2) & 31) * 16 + (o >> 7) * 8 + (o & 3), got).astype(BF16)
    o, k = iota((128, n), 0), iota((128, n), 1)
    near = ((o >> 2) & 15) * 16 + (o >> 6) * 8 + 4 + (o & 3)
    right = jnp.concatenate(
        [pick(k == near, got)[:, :64], pick(k == near + 256, got)[:, :64]], axis=1
    ).astype(BF16)
    r, lane = iota((n, 128), 0) & 15, iota((n, 128), 1)
    sums = jnp.where(lane >= 64, got.astype(F32), 0.0)
    for e in range(2):
        adam = whole_sum(jnp.where((r >= 8 * e + 4) & (r < 8 * e + 8), sums, 0.0))
        adam = jnp.where(iota((16, 128), 0) == 0, three_lanes(adam, (16, 128), 0), 0.0).astype(BF16)
        for dest in range(16):
            if (dest // 4) % 2 == e:
                out_ref[dest, 0:128] = pairs[128 * e : 128 * e + 128]
                out_ref[dest, 128:192] = right[64 * e : 64 * e + 64]
                out_ref[dest, 192:208] = adam


def block_kernel(coord_ref, own_ref, other_ref, out_ref, left, right, grad, parts):
    yh, x, c = coord_ref[1], coord_ref[2], coord_ref[3]
    sums = jnp.zeros((16, 128), F32)
    for yy in range(4):
        for xx in range(4):
            i = yy * 4 + xx
            rr, cc = slice(128 * yy, 128 * yy + 128), slice(128 * xx, 128 * xx + 128)
            a0, a1 = own_ref[i, 0:128, :], other_ref[i, 0:128, :]
            low = jnp.where(c == 0, a0[:, :64], a1[:, :64])
            high = jnp.where(c == 0, a1[:, :64], a0[:, :64])
            left[rr, cc] = jnp.concatenate([low, high], axis=1)
            grad[rr, cc] = jnp.concatenate([a0[:, 64:], a1[:, 64:]], axis=1)
            b0, b1 = own_ref[i, 128:192, :], other_ref[i, 128:192, :]
            mid = 128 * yy + 64
            right[128 * yy : mid, cc] = jnp.concatenate([b0[:, :64], b1[:, :64]], axis=1)
            right[mid : mid + 64, cc] = jnp.concatenate([b0[:, 64:], b1[:, 64:]], axis=1)
            sums = sums + own_ref[i, 192:208, :].astype(F32) + other_ref[i, 192:208, :].astype(F32)
    lanes = (((1,), (1,)), ((), ()))
    product = lax.dot_general(right[...], grad[...], lanes, preferred_element_type=F32).astype(BF16)
    shampoo = lax.dot_general(left[...], product, lanes, preferred_element_type=F32).astype(BF16)
    wide = shampoo.astype(F32)
    scale = jnp.sqrt(whole_sum(sums) / (whole_sum(wide * wide) + NORM_EPS))
    direction = (scale * wide).astype(BF16)
    for hh in range(2):
        for xx in range(4):
            parts[4 * hh + xx] = direction[256 * hh : 256 * hh + 256, 128 * xx : 128 * xx + 128]
    mine = parts[4 * yh + x]
    mine = jnp.where(c == 0, mine[:, :64], mine[:, 64:])
    out_ref[...] = jnp.concatenate([mine, three_lanes(scale, (256, 64), 0).astype(BF16)], axis=1)


def unpack_kernel(table_ref, in_ref, dir_ref, graft_ref):
    got = in_ref[...]
    rows = 4 * NB
    row = iota((rows, NB), 0)
    at = jnp.broadcast_to(table_ref[0:1, 0:NB], (rows, NB))
    s = total(iota((rows, NB), 1) == (row >> 2), at, 1)
    source = ((s & 1) * NZ + (s >> 1)) * 4 + (iota((rows, 1), 0) & 3)
    dir_ref[...] = pick(iota((rows, 256), 1) == source, got[:, :64]).astype(BF16)
    scales = jnp.sum(got[:, 64:].astype(F32), axis=1, keepdims=True)
    grafts = []
    for k in range(2):
        hit = iota((256, NB), 0) == table_ref[k + 1 : k + 2, 0:NB]
        grafts.append(whole_sum(jnp.where(hit, jnp.broadcast_to(scales, (256, NB)), 0.0)))
    graft_ref[...] = jnp.where(iota((1, 2), 1) == 0, grafts[0], grafts[1])


def per_device(gradient, second_moment, factors, old_owner, new_owner, offsets):
    rank = lax.axis_index(("yh", "yl", "z"))
    coords = jnp.stack([rank, lax.axis_index("yh"), lax.axis_index("x"), lax.axis_index("c")])
    coords = coords.astype(jnp.int32)
    old, own, off = (a.reshape(1, NB) for a in (old_owner, new_owner, offsets))
    params = pltpu.CompilerParams(vmem_limit_bytes=40 * 1024 * 1024)
    with jax.named_scope("pack"):
        moment_new, send, table = pl.pallas_call(
            pack_kernel,
            out_shape=(
                jax.ShapeDtypeStruct((4 * NB, 64), F32),
                jax.ShapeDtypeStruct((16 * NZ, 128), BF16),
                jax.ShapeDtypeStruct((8, 128), jnp.int32),
            ),
            in_specs=[SMEM] + [ANY] * 6,
            out_specs=(VMEM, VMEM, VMEM),
            scratch_shapes=[
                pltpu.VMEM((4 * NB, 64), BF16),
                pltpu.VMEM((4 * NB, 64), F32),
                pltpu.VMEM((8 * NB, 64), BF16),
                pltpu.VMEM((1, NB), jnp.int32),
                pltpu.VMEM((1, NB), jnp.int32),
                pltpu.VMEM((1, NB), jnp.int32),
                pltpu.SemaphoreType.DMA((6,)),
            ],
            compiler_params=pltpu.CompilerParams(vmem_limit_bytes=60 * 1024 * 1024),
        )(
            coords,
            gradient.reshape(4 * NB, 64),
            second_moment.reshape(4 * NB, 64),
            factors.reshape(8 * NB, 64),
            old,
            own,
            off,
        )
    with jax.named_scope("to_planes"):
        got = lax.all_to_all(send.reshape(NZ, 16, 128), "z", 0, 0, tiled=True)
    with jax.named_scope("spread"):
        send = pl.pallas_call(
            spread_kernel,
            out_shape=jax.ShapeDtypeStruct((16, 208, 128), BF16),
            in_specs=[VMEM],
            out_specs=VMEM,
            compiler_params=params,
        )(got.reshape(16 * NZ, 128))
    with jax.named_scope("in_plane"):
        got = lax.all_to_all(send, ("yh", "yl", "x"), 0, 0, tiled=True)
    with jax.named_scope("cores"):
        other = lax.ppermute(got, "c", [(0, 1), (1, 0)])
    with jax.named_scope("block"):
        send = pl.pallas_call(
            block_kernel,
            out_shape=jax.ShapeDtypeStruct((256, 128), BF16),
            in_specs=[SMEM, VMEM, VMEM],
            out_specs=VMEM,
            scratch_shapes=[pltpu.VMEM((512, 512), BF16)] * 3 + [pltpu.VMEM((8, 256, 128), BF16)],
            compiler_params=params,
        )(coords, got, other)
    with jax.named_scope("back"):
        got = lax.all_to_all(send.reshape(64, 4, 128), ("yl", "z"), 0, 0, tiled=True)
    with jax.named_scope("unpack"):
        direction, grafts = pl.pallas_call(
            unpack_kernel,
            out_shape=(
                jax.ShapeDtypeStruct((4 * NB, 64), BF16),
                jax.ShapeDtypeStruct((1, 2), F32),
            ),
            in_specs=[VMEM, VMEM],
            out_specs=(VMEM, VMEM),
            compiler_params=params,
        )(table, got.reshape(256, 128))
    return (direction.reshape(NB, 4, 64), moment_new.reshape(NB, 4, 64), grafts)


def solution(mesh):
    split = Mesh(mesh.devices.reshape(2, 2, NZ, 4, 2), ("yh", "yl", "z", "x", "c"))
    dp, tensor = ("yh", "yl", "z"), ("x", "c")
    flat = P(None, dp, tensor)
    return jax.shard_map(
        per_device,
        mesh=split,
        in_specs=(flat, flat, P(None, None, dp, tensor), P(), P(), P()),
        out_specs=(flat, flat, P(dp, None)),
        check_vma=False,
    )
```

time: 632 us -> 122 us (0.19)
  waiting for transfers between devices: 329 us -> 1.98 us
  blocking collectives: 218 us -> 106 us
  local copies, waits for them, and re-layouts: 35.1 us -> 0.01 us
  starting transfers between devices: 26.9 us -> 5.85 us
  between operations: 13.9 us -> 0.69 us
    all_gather x3 -> x0, waiting for transfers between devices: 300 us -> none  [the longest x1 225 us: per_device(): lax.all_gather(factors, 'dp', axis=2, tiled=True)[wanted]]
    psum x1 -> x0, blocking collectives: 151 us -> none  [per_device(): lax.psum((adam_sq[offsets], jnp.sum(wide_back * wide_back, axis=(1, 2))),...]
    all_to_all x1 -> x3, blocking collectives: 66.4 us -> 106 us  [the longest x1 58.9 us: per_device(): got = lax.all_to_all(send.reshape(NZ, 16, 128), 'z', 0, 0, tiled=True)]
    all_to_all x1 -> x0, waiting for transfers between devices: 29.4 us -> none  [per_device(): lax.all_to_all(returning, 'dp', split_axis=0, concat_axis=0, tiled=True)]
    all_to_all x1 -> x0, starting transfers between devices: 26.8 us -> none  [per_device(): lax.all_to_all(returning, 'dp', split_axis=0, concat_axis=0, tiled=True)]
    all_gather x1 -> x0, local copies, waits for them, and re-layouts: 16.2 us -> none  [per_device(): lax.all_gather(factors, 'dp', axis=2, tiled=True)[wanted]]
    gather x7 -> x0, local copies, waits for them, and re-layouts: 8.07 us -> none  [the longest x2 3.66 us: per_device(): lax.all_gather(factors, 'dp', axis=2, tiled=True)[wanted]]
  transfers between devices with their start and end apart: 4 -> 1, of which waited for: 4 -> 1; matrix products, arithmetic and copies ran while one was open for 5% -> 0% of each run, Pallas kernels for 0% -> 0%
where the time goes in v1:
time: 122 us; the launch traced here: 121 us
  blocking collectives  106 us (87%)
  Pallas kernels  6.15 us (5%)
  starting transfers between devices  5.85 us (5%)
  waiting for transfers between devices  1.98 us (2%)
    all_to_all x1, blocking collectives, per_device(): got = lax.all_to_all(send.reshape(NZ, 16, 128), 'z', 0, 0, tiled=True)  58.9 us
    all_to_all x1, blocking collectives, per_device(): lax.all_to_all(send.reshape(64, 4, 128), ('yl', 'z'), 0, 0, tiled=True)  28.2 us
    all_to_all x1, blocking collectives, per_device(): got = lax.all_to_all(send, ('yh', 'yl', 'x'), 0, 0, tiled=True)  18.7 us
    ppermute x1, starting transfers between devices, per_device(): other = lax.ppermute(got, 'c', [(0, 1), (1, 0)])  5.85 us
    pallas_call x1, Pallas kernels, per_device(): pl.pallas_call(pack_kernel, out_shape=(jax.ShapeDtypeStruct((4 * NB, 64),...  2.88 us
  transfers between devices with their start and end apart: 1, of which 1 were waited for; matrix products, arithmetic and copies ran while one was open for 0% of the time, Pallas kernels for 0%

profile of v1, /device:TPU:1, one launch (start us, length us, event | category | flops | bytes accessed | tf_op | source)
XLA Modules:
  0.0 121.1 jit_solution(13564781425303940133)
XLA Ops:
  0.6 0.6 pad_add_fusion.coord_ref
  1.3 2.9 %pack.1 = (f32[224,64]{1,0:T(8,128)}, bf16[512,128]{1,0:T(8,128)(2,1)}, s32[8,128]{1,0:T(8,128)}) custom-call(s32[4]{0:T(128)} %pad_add_fusion.coord_ref, bf16[224,64]{1,0:T(8,128)(2,1)} %bitcast.22, f32[224,64]{1,0:T(8,128)} %bitcast.20, bf16[448,64]{1,0:T(8,128)(2,1)} %bitcast.21, s32[1,56]{1,0:T(1,128)} %bitcast.23, s32[1,56]{1,0:T(1,128)} %bitcast.24, ...), custom_call_target="tpu_custom_call" | custom-call | tf_op jit(solution)/shard_map/pack/pallas_call | solution.py:200
  4.1 58.9 %all_to_all.15 = bf16[32,16,128]{2,1,0:T(8,128)(2,1)S(1)} all-to-all(bf16[32,16,128]{2,1,0:T(8,128)(2,1)} %bitcast.19), channel_id=1, replica_groups=mesh['yh'=2,'yl'=2,'z'=32,'x'=4,'c'=2] {'z'}, dimensions={0} | all-to-all | bytes 262144 | tf_op jit(solution)/shard_map/to_planes/all_to_all | solution.py:229
  63.0 0.5 spread.1
  63.5 0.0 copy-start
  63.5 18.7 %all_to_all.16.own_ref = bf16[16,208,128]{2,1,0:T(8,128)(2,1)S(1)} all-to-all(bf16[16,208,128]{2,1,0:T(8,128)(2,1)S(1)} %spread.1), channel_id=1, replica_groups=mesh['yh'=2,'yl'=2,'z'=32,'x'=4,'c'=2] {'yh','yl','x'}, dimensions={0} | all-to-all | bytes 1703936 | tf_op jit(solution)/shard_map/in_plane/all_to_all | solution.py:239
  82.2 5.8 %collective-permute-start = (bf16[16,208,128]{2,1,0:T(8,128)(2,1)S(1)}, bf16[16,208,128]{2,1,0:T(8,128)(2,1)S(1)}, u32[]{:S(2)}, u32[]{:S(2)}) collective-permute-start(bf16[16,208,128]{2,1,0:T(8,128)(2,1)S(1)} %all_to_all.16.own_ref), channel_id=1, source_target_pairs={{0,1},{1,0},{2,3},{3,2},{4,5},{5,4},{6,7},{7,6},{8,9},{9,8},{10,11... | collective-permute-start | bytes 2555912 | tf_op jit(solution)/shard_map/cores/ppermute | solution.py:241
  88.1 2.0 %collective-permute-done.other_ref = bf16[16,208,128]{2,1,0:T(8,128)(2,1)S(1)} collective-permute-done((bf16[16,208,128]{2,1,0:T(8,128)(2,1)S(1)}, bf16[16,208,128]{2,1,0:T(8,128)(2,1)S(1)}, u32[]{:S(2)}, u32[]{:S(2)}) %collective-permute-start) | collective-permute-done | bytes 852000 | tf_op jit(solution)/shard_map/cores/ppermute | solution.py:241
  90.1 0.0 copy-done
  90.1 1.9 %block.1 = bf16[256,128]{1,0:T(8,128)(2,1)S(1)} custom-call(s32[4]{0:T(128)S(1)} %copy-done, bf16[16,208,128]{2,1,0:T(8,128)(2,1)S(1)} %all_to_all.16.own_ref, bf16[16,208,128]{2,1,0:T(8,128)(2,1)S(1)} %collective-permute-done.other_ref), custom_call_target="tpu_custom_call" | custom-call | tf_op jit(solution)/shard_map/block/pallas_call | solution.py:243
  92.0 0.0 copy-start.1
  92.0 28.2 %all_to_all.17 = bf16[64,4,128]{2,1,0:T(4,128)(2,1)S(1)} all-to-all(bf16[64,4,128]{2,1,0:T(4,128)(2,1)S(1)} %bitcast.18), channel_id=1, replica_groups=mesh['yh'=2,'yl'=2,'z'=32,'x'=4,'c'=2] {'yl','z'}, dimensions={0} | all-to-all | bytes 131072 | tf_op jit(solution)/shard_map/back/all_to_all | solution.py:252
  120.2 0.0 copy-done.1
  120.2 0.9 unpack.1
Async XLA Ops:
  63.5 26.5 %copy-start = (s32[4]{0:T(128)S(1)}, s32[4]{0:T(128)}, u32[]{:S(2)}) copy-start(s32[4]{0:T(128)} %pad_add_fusion.coord_ref) | copy-start | bytes 52
  82.2 7.8 %collective-permute-start = (bf16[16,208,128]{2,1,0:T(8,128)(2,1)S(1)}, bf16[16,208,128]{2,1,0:T(8,128)(2,1)S(1)}, u32[]{:S(2)}, u32[]{:S(2)}) collective-permute-start(bf16[16,208,128]{2,1,0:T(8,128)(2,1)S(1)} %all_to_all.16.own_ref), channel_id=1, source_target_pairs={{0,1},{1,0},{2,3},{3,2},{4,5},{5,4},{6,7},{7,6},{8,9},{9,8},{10,11... | collective-permute-start | bytes 2555912 | tf_op jit(solution)/shard_map/cores/ppermute | solution.py:241
  92.0 28.2 %copy-start.1 = (s32[8,128]{1,0:T(8,128)S(1)}, s32[8,128]{1,0:T(8,128)}, u32[]{:S(2)}) copy-start(s32[8,128]{1,0:T(8,128)} %get-tuple-element.8.table_ref) | copy-start | bytes 12292

commit v2 on v1

v2 whole, which is shorter than its diff:
```python
import jax
import jax.numpy as jnp
from jax import lax
from jax.experimental import pallas as pl
from jax.experimental.pallas import tpu as pltpu
from jax.sharding import Mesh
from jax.sharding import PartitionSpec as P

BETA_TWO = 0.99
ADAM_EPS = 1e-08
NORM_EPS = 1e-06
F32 = jnp.float32
BF16 = jnp.bfloat16
NB = 56
NZ = 32
SENDROWS = 10
PLANE_FACTOR = 6554
VMEM = pl.BlockSpec(memory_space=pltpu.VMEM)
ANY = pl.BlockSpec(memory_space=pl.ANY)


def iota(shape, dim):
    return lax.broadcasted_iota(jnp.int32, shape, dim)


def total(mask, values, axis):
    picked = jnp.where(mask, values.astype(F32), 0.0)
    return jnp.sum(picked, axis=axis, keepdims=True).astype(jnp.int32)


def one_hot(mask):
    return jnp.where(mask, 1.0, 0.0).astype(BF16)


def pick(mask, rows):
    return jnp.dot(one_hot(mask), rows, preferred_element_type=F32)


def to_column(row):
    sub, lane = iota((NB, NB), 0), iota((NB, NB), 1)
    return total(sub == lane, jnp.broadcast_to(row, (NB, NB)), 1)


def to_column_wide(row):
    sub, lane = iota((NB, NB), 0), iota((NB, NB), 1)
    return jnp.sum(jnp.where(sub == lane, jnp.broadcast_to(row, (NB, NB)), 0.0), axis=1, keepdims=True)


def tied_before(row, column):
    sub, lane = iota((NB, NB), 0), iota((NB, NB), 1)
    return total((column == row) & (sub < lane), jnp.ones((NB, NB), jnp.int32), 0)


def slots_row(row, column):
    sub, lane = iota((NB, NB), 0), iota((NB, NB), 1)
    before = (column < row) | ((column == row) & (sub < lane))
    return total(before, jnp.ones((NB, NB), jnp.int32), 0)


def split_three(x):
    high = x.astype(BF16).astype(F32)
    rest = x - high
    mid = rest.astype(BF16).astype(F32)
    return high, mid, (rest - mid).astype(BF16).astype(F32)


def three_lanes(x, lane):
    high, mid, low = split_three(x)
    return jnp.where(lane == 0, high, jnp.where(lane == 1, mid, jnp.where(lane == 2, low, 0.0)))


def whole_sum(x):
    return jnp.sum(jnp.sum(x, axis=0, keepdims=True), axis=1, keepdims=True)


def adam_moment(grad, moment):
    wide = grad.astype(F32)
    return wide, BETA_TWO * moment + (1.0 - BETA_TWO) * wide * wide


def dp_rank():
    return (lax.axis_index("yh") * 2 + lax.axis_index("yl")) * NZ + lax.axis_index("z")


def fetch(pairs, sems):
    copies = [pltpu.make_async_copy(src, dst, sems.at[i]) for i, (src, dst) in enumerate(pairs)]
    for copy in copies:
        copy.start()
    return copies


def pack_kernel(
    grad_hbm, moment_hbm, factor_hbm, old_hbm, off_hbm, send_ref,
    grad_ref, moment_ref, factor_ref, old_ref, off_ref, sems,
):
    copies = fetch(
        (
            (old_hbm, old_ref),
            (off_hbm, off_ref),
            (grad_hbm, grad_ref),
            (moment_hbm, moment_ref),
            (factor_hbm, factor_ref),
        ),
        sems,
    )
    row0 = dp_rank() * 4
    col0 = (lax.axis_index("x") * 2 + lax.axis_index("c")) * 64
    for copy in copies[:2]:
        copy.wait()
    old = old_ref[...]
    slot_col, off_col = to_column(slots_row(old, to_column(old))), to_column(off_ref[...])
    position = total(slot_col == iota((NB, NB), 1), jnp.broadcast_to(off_col, (NB, NB)), 0)
    rows = SENDROWS * NZ
    sent = iota((rows, NB), 0)
    plane = (sent * PLANE_FACTOR) >> 16
    q = sent - SENDROWS * plane
    seat = 2 * plane + ((q >> 2) & 1)
    spread = total(iota((rows, NB), 1) == seat, jnp.broadcast_to(position, (rows, NB)), 1)
    plane, q = plane[:, 0:1], q[:, 0:1]
    r = q & 3
    from_factor = jnp.where(q < 8, (2 * plane + (q >> 2)) * 8 + r, -1)
    from_grad = jnp.where(q < 8, spread * 4 + r, jnp.where(q == 8, 4 * NB + plane, -1)) + 8 * NB
    k = iota((rows, 12 * NB + NZ), 1)
    mask = (k == from_factor) | (k == from_grad)
    for copy in copies[2:]:
        copy.wait()
    grad = grad_ref[...]
    wide, moment = adam_moment(grad, moment_ref[...])
    step = wide / (jnp.sqrt(moment) + ADAM_EPS)
    by_row = jnp.sum(step * step, axis=1, keepdims=True)
    mine = iota((4 * NB, NB), 1) == (iota((4 * NB, NB), 0) >> 2)
    by_block = jnp.sum(jnp.where(mine, by_row, 0.0), axis=0, keepdims=True)
    by_slot = jnp.sum(
        jnp.where(
            iota((NB, NB), 0) == jnp.broadcast_to(position, (NB, NB)), to_column_wide(by_block), 0.0
        ),
        axis=0,
        keepdims=True,
    )
    factor = factor_ref[...].astype(F32)
    r8, lane = iota((8 * NB, 64), 0) & 7, iota((8 * NB, 64), 1)
    row, col = row0 + (r8 & 3), col0 + lane
    right = pltpu.roll(factor, 8 * NB - 4, 0)
    mixed = jnp.where(col > row, factor, right)
    on_diagonal = jnp.sum(jnp.where((col == row) & (r8 < 4), factor, 0.0), axis=1, keepdims=True)
    r8, lane = iota((8 * NB, 128), 0), iota((8 * NB, 128), 1)
    seat_lane = 64 * ((r8 >> 3) & 1) + 8 + (r8 & 3)
    on_diagonal = jnp.where(lane == seat_lane, on_diagonal, 0.0).astype(BF16)
    extra = pick(iota((NZ, 8 * NB), 0) == (iota((NZ, 8 * NB), 1) >> 4), on_diagonal)
    p, s = iota((NZ, NB), 0), iota((NZ, NB), 1)
    for e in range(2):
        adam = jnp.sum(jnp.where(s == 2 * p + e, by_slot, 0.0), axis=1, keepdims=True)
        extra = extra + three_lanes(adam, iota((NZ, 128), 1) - 64 * e)
    none = jnp.zeros((8 * NB, 64), BF16)
    source = jnp.concatenate(
        [
            jnp.concatenate([mixed.astype(BF16), none], axis=1),
            jnp.concatenate([none[: 4 * NB], grad], axis=1),
            extra.astype(BF16),
        ],
        axis=0,
    )
    send_ref[...] = pick(mask, source).astype(BF16)


def moment_kernel(
    after_hbm, grad_hbm, moment_hbm, old_hbm, own_hbm, off_hbm, new_ref, table_ref,
    grad_ref, moment_ref, old_ref, own_ref, off_ref, sems,
):
    del after_hbm
    copies = fetch(
        (
            (old_hbm, old_ref),
            (off_hbm, off_ref),
            (own_hbm, own_ref),
            (grad_hbm, grad_ref),
            (moment_hbm, moment_ref),
        ),
        sems,
    )
    for copy in copies:
        copy.wait()
    new_ref[...] = adam_moment(grad_ref[...], moment_ref[...])[1]
    old, own = old_ref[...], own_ref[...]
    slot = slots_row(old, to_column(old))
    slot_col, off_col = to_column(slot), to_column(off_ref[...])
    at = total(off_col == iota((NB, NB), 1), jnp.broadcast_to(slot_col, (NB, NB)), 0)
    rank = tied_before(own, to_column(own))
    held = own == dp_rank()
    first_row = ((slot & 1) * NZ + (slot >> 1)) * 4
    table_ref[0:1, 0:NB] = at
    for k in range(2):
        table_ref[k + 1 : k + 2, 0:NB] = jnp.where(held & (rank == k), first_row, -1)


def spread_kernel(in_ref, out_ref):
    n = SENDROWS * NZ
    got = in_ref[...]
    o, k = iota((256, n), 0), iota((256, n), 1)
    pairs = pick(k == ((o >> 2) & 31) * SENDROWS + (o >> 7) * 4 + (o & 3), got).astype(BF16)
    o, k = iota((NZ, n), 0), iota((NZ, n), 1)
    extra = pick(k == o * SENDROWS + 8, got).astype(BF16)
    for e in range(2):
        lanes = slice(64 * e, 64 * e + 64)
        rest = jnp.concatenate([extra[:16, lanes], extra[16:, lanes]], axis=1)
        for dest in range(16):
            if (dest // 4) % 2 == e:
                out_ref[dest, 0:128] = pairs[128 * e : 128 * e + 128]
                out_ref[dest, 128:144] = rest


def block_kernel(own_ref, other_ref, table_hbm, out_ref, mixed, grad, parts):
    del table_hbm
    yh, x, c = lax.axis_index("yh"), lax.axis_index("x"), lax.axis_index("c")

    def assemble(low_ref, high_ref):
        for yy in range(4):
            for xx in range(4):
                i = yy * 4 + xx
                rr, cc = slice(128 * yy, 128 * yy + 128), slice(128 * xx, 128 * xx + 128)
                low, high = low_ref[i, 0:128, :], high_ref[i, 0:128, :]
                mixed[rr, cc] = jnp.concatenate([low[:, :64], high[:, :64]], axis=1)
                grad[rr, cc] = jnp.concatenate([low[:, 64:], high[:, 64:]], axis=1)

    @pl.when(c == 0)
    def _():
        assemble(own_ref, other_ref)

    @pl.when(c == 1)
    def _():
        assemble(other_ref, own_ref)

    extras = []
    for yy in range(4):
        parts_of = [ref[4 * yy + xx, 128:144, :].astype(F32) for ref in (own_ref, other_ref) for xx in range(4)]
        extras.append(sum(parts_of[1:], parts_of[0]))
    extra = jnp.concatenate(extras, axis=0)
    lane = iota((64, 128), 1) & 63
    adam_sq = whole_sum(jnp.where(lane < 3, extra, 0.0))
    diagonal = jnp.where(lane < 3, 0.0, extra).astype(BF16)
    i, k = iota((512, 64), 0), iota((512, 64), 1)
    diagonal = pick(k == ((i >> 7) * 16 + ((i >> 2) & 15)), diagonal)
    i, k = iota((512, 128), 0), iota((512, 128), 1)
    seat_lane = ((i >> 6) & 1) * 64 + 8 + (i & 3)
    diagonal = jnp.sum(jnp.where(k == seat_lane, diagonal, 0.0), axis=1, keepdims=True)
    entries = mixed[...].astype(F32)
    turned = entries.T
    row, col = iota((512, 512), 0), iota((512, 512), 1)
    left = jnp.where(col > row, entries, jnp.where(col < row, turned, diagonal)).astype(BF16)
    right = jnp.where(col > row, turned, entries).astype(BF16)
    lanes = (((1,), (1,)), ((), ()))
    product = lax.dot_general(right, grad[...], lanes, preferred_element_type=F32).astype(BF16)
    shampoo = lax.dot_general(left, product, lanes, preferred_element_type=F32).astype(BF16)
    wide = shampoo.astype(F32)
    scale = jnp.sqrt(adam_sq / (whole_sum(wide * wide) + NORM_EPS))
    direction = (scale * wide).astype(BF16)
    for hh in range(2):
        for xx in range(4):
            parts[4 * hh + xx] = direction[256 * hh : 256 * hh + 256, 128 * xx : 128 * xx + 128]
    mine = parts[4 * yh + x]
    mine = jnp.where(c == 0, mine[:, :64], mine[:, 64:])
    out_ref[...] = jnp.concatenate([mine, three_lanes(scale, iota((256, 64), 1)).astype(BF16)], axis=1)


def unpack_kernel(table_ref, in_ref, dir_ref, graft_ref):
    got = in_ref[...]
    rows = 4 * NB
    row = iota((rows, NB), 0)
    at = jnp.broadcast_to(table_ref[0:1, 0:NB], (rows, NB))
    s = total(iota((rows, NB), 1) == (row >> 2), at, 1)
    source = ((s & 1) * NZ + (s >> 1)) * 4 + (iota((rows, 1), 0) & 3)
    dir_ref[...] = pick(iota((rows, 256), 1) == source, got[:, :64]).astype(BF16)
    scales = jnp.sum(got[:, 64:].astype(F32), axis=1, keepdims=True)
    grafts = []
    for k in range(2):
        hit = iota((256, NB), 0) == table_ref[k + 1 : k + 2, 0:NB]
        grafts.append(whole_sum(jnp.where(hit, jnp.broadcast_to(scales, (256, NB)), 0.0)))
    graft_ref[...] = jnp.where(iota((1, 2), 1) == 0, grafts[0], grafts[1])


def per_device(gradient, second_moment, factors, old_owner, new_owner, offsets):
    old, own, off = (a.reshape(1, NB) for a in (old_owner, new_owner, offsets))
    grad, moment = gradient.reshape(4 * NB, 64), second_moment.reshape(4 * NB, 64)
    params = pltpu.CompilerParams(vmem_limit_bytes=40 * 1024 * 1024)
    wide_params = pltpu.CompilerParams(vmem_limit_bytes=60 * 1024 * 1024)
    index = pltpu.VMEM((1, NB), jnp.int32)
    with jax.named_scope("pack"):
        send = pl.pallas_call(
            pack_kernel,
            out_shape=jax.ShapeDtypeStruct((SENDROWS * NZ, 128), BF16),
            in_specs=[ANY] * 5,
            out_specs=VMEM,
            scratch_shapes=[
                pltpu.VMEM((4 * NB, 64), BF16),
                pltpu.VMEM((4 * NB, 64), F32),
                pltpu.VMEM((8 * NB, 64), BF16),
                index,
                index,
                pltpu.SemaphoreType.DMA((5,)),
            ],
            compiler_params=wide_params,
        )(grad, moment, factors.reshape(8 * NB, 64), old, off)
    with jax.named_scope("to_planes"):
        got = lax.all_to_all(send.reshape(NZ * SENDROWS // 2, 2, 128), "z", 0, 0, tiled=True)
    with jax.named_scope("spread"):
        send = pl.pallas_call(
            spread_kernel,
            out_shape=jax.ShapeDtypeStruct((16, 144, 128), BF16),
            in_specs=[VMEM],
            out_specs=VMEM,
            compiler_params=params,
        )(got.reshape(SENDROWS * NZ, 128))
    with jax.named_scope("in_plane"):
        got = lax.all_to_all(send, ("yh", "yl", "x"), 0, 0, tiled=True)
    with jax.named_scope("cores"):
        other = lax.ppermute(got, "c", [(0, 1), (1, 0)])
    with jax.named_scope("moment"):
        moment_new, table = pl.pallas_call(
            moment_kernel,
            out_shape=(
                jax.ShapeDtypeStruct((4 * NB, 64), F32),
                jax.ShapeDtypeStruct((8, 128), jnp.int32),
            ),
            in_specs=[ANY] * 6,
            out_specs=(VMEM, VMEM),
            scratch_shapes=[
                pltpu.VMEM((4 * NB, 64), BF16),
                pltpu.VMEM((4 * NB, 64), F32),
                index,
                index,
                index,
                pltpu.SemaphoreType.DMA((5,)),
            ],
            compiler_params=params,
        )(got, grad, moment, old, own, off)
    with jax.named_scope("block"):
        send = pl.pallas_call(
            block_kernel,
            out_shape=jax.ShapeDtypeStruct((256, 128), BF16),
            in_specs=[VMEM, VMEM, ANY],
            out_specs=VMEM,
            scratch_shapes=[pltpu.VMEM((512, 512), BF16)] * 2 + [pltpu.VMEM((8, 256, 128), BF16)],
            compiler_params=params,
        )(got, other, table)
    with jax.named_scope("back"):
        got = lax.all_to_all(send.reshape(64, 4, 128), ("yl", "z"), 0, 0, tiled=True)
    with jax.named_scope("unpack"):
        direction, grafts = pl.pallas_call(
            unpack_kernel,
            out_shape=(
                jax.ShapeDtypeStruct((4 * NB, 64), BF16),
                jax.ShapeDtypeStruct((1, 2), F32),
            ),
            in_specs=[VMEM, VMEM],
            out_specs=(VMEM, VMEM),
            compiler_params=params,
        )(table, got.reshape(256, 128))
    return (direction.reshape(NB, 4, 64), moment_new.reshape(NB, 4, 64), grafts)


def solution(mesh):
    split = Mesh(mesh.devices.reshape(2, 2, NZ, 4, 2), ("yh", "yl", "z", "x", "c"))
    dp, tensor = ("yh", "yl", "z"), ("x", "c")
    flat = P(None, dp, tensor)
    return jax.shard_map(
        per_device,
        mesh=split,
        in_specs=(flat, flat, P(None, None, dp, tensor), P(), P(), P()),
        out_specs=(flat, flat, P(dp, None)),
        check_vma=False,
    )
```

time: 122 us -> 113 us (0.926)
  blocking collectives: 106 us -> 98.7 us
  waiting for transfers between devices: 1.98 us -> 0.5 us
    all_to_all x1, blocking collectives: 58.9 us -> 54.2 us  [per_device(): lax.all_to_all(send.reshape(NZ * SENDROWS // 2, 2, 128), 'z', 0, 0, tiled...]
    all_to_all x1, blocking collectives: 18.7 us -> 16.6 us  [per_device(): got = lax.all_to_all(send, ('yh', 'yl', 'x'), 0, 0, tiled=True)]
    ppermute x1, waiting for transfers between devices: 1.98 us -> 0.5 us  [per_device(): other = lax.ppermute(got, 'c', [(0, 1), (1, 0)])]
    pallas_call x2 -> x3, Pallas kernels: 3.34 us -> 3.94 us  [the longest x1 2.6 us: per_device(): pl.pallas_call(pack_kernel, out_shape=jax.ShapeDtypeStruct((SENDROWS * NZ...]
  transfers between devices with their start and end apart: 1 -> 1, of which waited for: 1 -> 1; matrix products, arithmetic and copies ran while one was open for 0% -> 0% of each run, Pallas kernels for 0% -> 1%
where the time goes in v2:
time: 113 us
  blocking collectives  98.7 us (87%)
  Pallas kernels  6.39 us (6%)
  starting transfers between devices  6.22 us (6%)
    all_to_all x1, blocking collectives, per_device(): lax.all_to_all(send.reshape(NZ * SENDROWS // 2, 2, 128), 'z', 0, 0, tiled...  54.2 us
    all_to_all x1, blocking collectives, per_device(): lax.all_to_all(send.reshape(64, 4, 128), ('yl', 'z'), 0, 0, tiled=True)  27.9 us
    all_to_all x1, blocking collectives, per_device(): got = lax.all_to_all(send, ('yh', 'yl', 'x'), 0, 0, tiled=True)  16.6 us
    ppermute x1, starting transfers between devices, per_device(): other = lax.ppermute(got, 'c', [(0, 1), (1, 0)])  6.22 us
    pallas_call x1, Pallas kernels, per_device(): pl.pallas_call(pack_kernel, out_shape=jax.ShapeDtypeStruct((SENDROWS * NZ...  2.6 us
  transfers between devices with their start and end apart: 1, of which 1 were waited for; matrix products, arithmetic and copies ran while one was open for 0% of the time, Pallas kernels for 1%

profile of v2, /device:TPU:1, one launch (start us, length us, event | category | flops | bytes accessed | tf_op | source)
XLA Modules:
  0.0 112.6 jit_solution(8331780514863152519)
XLA Ops:
  0.6 2.6 %pack.1 = bf16[320,128]{1,0:T(8,128)(2,1)} custom-call(bf16[224,64]{1,0:T(8,128)(2,1)} %bitcast.17, f32[224,64]{1,0:T(8,128)} %bitcast.12, bf16[448,64]{1,0:T(8,128)(2,1)} %bitcast.25, s32[1,56]{1,0:T(1,128)} %bitcast.19, s32[1,56]{1,0:T(1,128)} %bitcast.21), custom_call_target="tpu_custom_call" | custom-call | tf_op jit(solution)/shard_map/pack/pallas_call | solution.py:288
  3.2 54.2 %all_to_all.15 = bf16[160,2,128]{2,1,0:T(2,128)(2,1)S(1)} all-to-all(bf16[160,2,128]{2,1,0:T(2,128)(2,1)} %bitcast.24), channel_id=1, replica_groups=mesh['yh'=2,'yl'=2,'z'=32,'x'=4,'c'=2] {'z'}, dimensions={0} | all-to-all | bytes 163840 | tf_op jit(solution)/shard_map/to_planes/all_to_all | solution.py:304
  57.4 0.3 spread.1
  57.7 0.0 copy-start
  57.7 0.0 copy-start.1
  57.7 16.6 %all_to_all.16.after_hbm.own_ref = bf16[16,144,128]{2,1,0:T(8,128)(2,1)S(1)} all-to-all(bf16[16,144,128]{2,1,0:T(8,128)(2,1)S(1)} %spread.1), channel_id=1, replica_groups=mesh['yh'=2,'yl'=2,'z'=32,'x'=4,'c'=2] {'yh','yl','x'}, dimensions={0} | all-to-all | bytes 1179648 | tf_op jit(solution)/shard_map/in_plane/all_to_all | solution.py:314
  74.4 0.0 copy-start.2
  74.4 0.0 copy-start.3
  74.4 0.0 copy-start.4
  74.4 6.2 %collective-permute-start = (bf16[16,144,128]{2,1,0:T(8,128)(2,1)S(1)}, bf16[16,144,128]{2,1,0:T(8,128)(2,1)S(1)}, u32[]{:S(2)}, u32[]{:S(2)}) collective-permute-start(bf16[16,144,128]{2,1,0:T(8,128)(2,1)S(1)} %all_to_all.16.after_hbm.own_ref), channel_id=1, source_target_pairs={{0,1},{1,0},{2,3},{3,2},{4,5},{5,4},{6,7},{7,6},{8,9},{9,8},{10,11... | collective-permute-start | bytes 1769480 | tf_op jit(solution)/shard_map/cores/ppermute | solution.py:316
  80.6 0.0 copy-done
  80.6 0.0 copy-done.1
  80.6 0.0 copy-done.2
  80.6 0.0 copy-done.3
  80.6 0.0 copy-done.4
  80.7 1.1 moment.1
  81.7 0.5 collective-permute-done.other_ref
  82.2 1.6 %block.1 = bf16[256,128]{1,0:T(8,128)(2,1)S(1)} custom-call(bf16[16,144,128]{2,1,0:T(8,128)(2,1)S(1)} %all_to_all.16.after_hbm.own_ref, bf16[16,144,128]{2,1,0:T(8,128)(2,1)S(1)} %collective-permute-done.other_ref, s32[8,128]{1,0:T(8,128)S(1)} %get-tuple-element.7.table_hbm.table_ref), custom_call_target="tpu_custom_call" | custom-call | tf_op jit(solution)/shard_map/block/pallas_call | solution.py:337
  83.8 27.9 %all_to_all.17 = bf16[64,4,128]{2,1,0:T(4,128)(2,1)S(1)} all-to-all(bf16[64,4,128]{2,1,0:T(4,128)(2,1)S(1)} %bitcast.15), channel_id=1, replica_groups=mesh['yh'=2,'yl'=2,'z'=32,'x'=4,'c'=2] {'yl','z'}, dimensions={0} | all-to-all | bytes 131072 | tf_op jit(solution)/shard_map/back/all_to_all | solution.py:346
  111.7 0.9 unpack.1
Async XLA Ops:
  57.7 22.9 %copy-start = (f32[56,4,64]{2,1,0:T(4,128)S(1)}, f32[56,4,64]{2,1,0:T(4,128)}, u32[]{:S(2)}) copy-start(f32[56,4,64]{2,1,0:T(4,128)} %param.7) | copy-start | bytes 172036
  57.7 22.9 %copy-start.1 = (bf16[56,4,64]{2,1,0:T(4,128)(2,1)S(1)}, bf16[56,4,64]{2,1,0:T(4,128)(2,1)}, u32[]{:S(2)}) copy-start(bf16[56,4,64]{2,1,0:T(4,128)(2,1)} %param.6) | copy-start | bytes 86020
  74.4 6.3 %copy-start.2 = (s32[56]{0:T(128)S(1)}, s32[56]{0:T(128)}, u32[]{:S(2)}) copy-start(s32[56]{0:T(128)} %param.9) | copy-start | bytes 676
  74.4 6.3 %copy-start.3 = (s32[56]{0:T(128)S(1)}, s32[56]{0:T(128)}, u32[]{:S(2)}) copy-start(s32[56]{0:T(128)} %param.11) | copy-start | bytes 676
  74.4 6.3 %copy-start.4 = (s32[56]{0:T(128)S(1)}, s32[56]{0:T(128)}, u32[]{:S(2)}) copy-start(s32[56]{0:T(128)} %param.10) | copy-start | bytes 676
  74.4 7.8 %collective-permute-start = (bf16[16,144,128]{2,1,0:T(8,128)(2,1)S(1)}, bf16[16,144,128]{2,1,0:T(8,128)(2,1)S(1)}, u32[]{:S(2)}, u32[]{:S(2)}) collective-permute-start(bf16[16,144,128]{2,1,0:T(8,128)(2,1)S(1)} %all_to_all.16.after_hbm.own_ref), channel_id=1, source_target_pairs={{0,1},{1,0},{2,3},{3,2},{4,5},{5,4},{6,7},{7,6},{8,9},{9,8},{10,11... | collective-permute-start | bytes 1769480 | tf_op jit(solution)/shard_map/cores/ppermute | solution.py:316

commit v3 on v2

--- a/solution.py
+++ b/solution.py
@@ -15,6 +15,9 @@
 NZ = 32
 SENDROWS = 10
 PLANE_FACTOR = 6554
+FIRST = 20
+ALONG_Z = [[(k + FIRST) % NZ for k in range(NZ)]]
+ALONG_YZ = [[y * NZ + (k + FIRST) % NZ for y in range(2) for k in range(NZ)]]
 VMEM = pl.BlockSpec(memory_space=pltpu.VMEM)
 ANY = pl.BlockSpec(memory_space=pl.ANY)
 
@@ -76,6 +79,14 @@
 def adam_moment(grad, moment):
     wide = grad.astype(F32)
     return wide, BETA_TWO * moment + (1.0 - BETA_TWO) * wide * wide
+
+
+def place(z):
+    return (z + (NZ - FIRST)) & (NZ - 1)
+
+
+def seat_row(slot):
+    return ((slot & 1) * NZ + place(slot >> 1)) * 4
 
 
 def dp_rank():
@@ -112,14 +123,16 @@
     position = total(slot_col == iota((NB, NB), 1), jnp.broadcast_to(off_col, (NB, NB)), 0)
     rows = SENDROWS * NZ
     sent = iota((rows, NB), 0)
-    plane = (sent * PLANE_FACTOR) >> 16
-    q = sent - SENDROWS * plane
+    group = (sent * PLANE_FACTOR) >> 16
+    q = sent - SENDROWS * group
+    plane = (group + FIRST) & (NZ - 1)
     seat = 2 * plane + ((q >> 2) & 1)
     spread = total(iota((rows, NB), 1) == seat, jnp.broadcast_to(position, (rows, NB)), 1)
     plane, q = plane[:, 0:1], q[:, 0:1]
     r = q & 3
-    from_factor = jnp.where(q < 8, (2 * plane + (q >> 2)) * 8 + r, -1)
-    from_grad = jnp.where(q < 8, spread * 4 + r, jnp.where(q == 8, 4 * NB + plane, -1)) + 8 * NB
+    used = (q < 8) & (plane < NB // 2)
+    from_factor = jnp.where(used, (2 * plane + (q >> 2)) * 8 + r, -1)
+    from_grad = jnp.where(used, spread * 4 + r, jnp.where(q == 8, 4 * NB + plane, -9 * NB)) + 8 * NB
     k = iota((rows, 12 * NB + NZ), 1)
     mask = (k == from_factor) | (k == from_grad)
     for copy in copies[2:]:
@@ -187,7 +200,7 @@
     at = total(off_col == iota((NB, NB), 1), jnp.broadcast_to(slot_col, (NB, NB)), 0)
     rank = tied_before(own, to_column(own))
     held = own == dp_rank()
-    first_row = ((slot & 1) * NZ + (slot >> 1)) * 4
+    first_row = seat_row(slot)
     table_ref[0:1, 0:NB] = at
     for k in range(2):
         table_ref[k + 1 : k + 2, 0:NB] = jnp.where(held & (rank == k), first_row, -1)
@@ -197,9 +210,9 @@
     n = SENDROWS * NZ
     got = in_ref[...]
     o, k = iota((256, n), 0), iota((256, n), 1)
-    pairs = pick(k == ((o >> 2) & 31) * SENDROWS + (o >> 7) * 4 + (o & 3), got).astype(BF16)
+    pairs = pick(k == place((o >> 2) & 31) * SENDROWS + (o >> 7) * 4 + (o & 3), got).astype(BF16)
     o, k = iota((NZ, n), 0), iota((NZ, n), 1)
-    extra = pick(k == o * SENDROWS + 8, got).astype(BF16)
+    extra = pick(k == place(o) * SENDROWS + 8, got).astype(BF16)
     for e in range(2):
         lanes = slice(64 * e, 64 * e + 64)
         rest = jnp.concatenate([extra[:16, lanes], extra[16:, lanes]], axis=1)
@@ -259,6 +272,8 @@
             parts[4 * hh + xx] = direction[256 * hh : 256 * hh + 256, 128 * xx : 128 * xx + 128]
     mine = parts[4 * yh + x]
     mine = jnp.where(c == 0, mine[:, :64], mine[:, 64:])
+    at = 4 * FIRST
+    mine = jnp.concatenate([mine[at:128], mine[:at], mine[128 + at :], mine[128 : 128 + at]], axis=0)
     out_ref[...] = jnp.concatenate([mine, three_lanes(scale, iota((256, 64), 1)).astype(BF16)], axis=1)
 
 
@@ -268,7 +283,7 @@
     row = iota((rows, NB), 0)
     at = jnp.broadcast_to(table_ref[0:1, 0:NB], (rows, NB))
     s = total(iota((rows, NB), 1) == (row >> 2), at, 1)
-    source = ((s & 1) * NZ + (s >> 1)) * 4 + (iota((rows, 1), 0) & 3)
+    source = seat_row(s) + (iota((rows, 1), 0) & 3)
     dir_ref[...] = pick(iota((rows, 256), 1) == source, got[:, :64]).astype(BF16)
     scales = jnp.sum(got[:, 64:].astype(F32), axis=1, keepdims=True)
     grafts = []
@@ -301,7 +316,7 @@
             compiler_params=wide_params,
         )(grad, moment, factors.reshape(8 * NB, 64), old, off)
     with jax.named_scope("to_planes"):
-        got = lax.all_to_all(send.reshape(NZ * SENDROWS // 2, 2, 128), "z", 0, 0, tiled=True)
+        got = lax.all_to_all(send.reshape(NZ * SENDROWS // 2, 2, 128), "z", 0, 0, tiled=True, axis_index_groups=ALONG_Z)
     with jax.named_scope("spread"):
         send = pl.pallas_call(
             spread_kernel,
@@ -343,7 +358,7 @@
             compiler_params=params,
         )(got, other, table)
     with jax.named_scope("back"):
-        got = lax.all_to_all(send.reshape(64, 4, 128), ("yl", "z"), 0, 0, tiled=True)
+        got = lax.all_to_all(send.reshape(64, 4, 128), ("yl", "z"), 0, 0, tiled=True, axis_index_groups=ALONG_YZ)
     with jax.named_scope("unpack"):
         direction, grafts = pl.pallas_call(
             unpack_kernel,

time: 113 us -> 103 us (0.912)
  blocking collectives: 98.7 us -> 90 us
  starting transfers between devices: 6.22 us -> 4.75 us
    all_to_all x1, blocking collectives: 54.2 us -> 43.6 us  [per_device(): lax.all_to_all(send.reshape(NZ * SENDROWS // 2, 2, 128), 'z', 0, 0, tiled...]
    ppermute x1, starting transfers between devices: 6.22 us -> 4.75 us  [per_device(): other = lax.ppermute(got, 'c', [(0, 1), (1, 0)])]
    all_to_all x1, blocking collectives: 27.9 us -> 29.2 us  [per_device(): lax.all_to_all(send.reshape(64, 4, 128), ('yl', 'z'), 0, 0, tiled=True, a...]
where the time goes in v3:
time: 103 us; the launch traced here: 102 us
  blocking collectives  90 us (87%)
  Pallas kernels  6.41 us (6%)
  starting transfers between devices  4.75 us (5%)
    all_to_all x1, blocking collectives, per_device(): lax.all_to_all(send.reshape(NZ * SENDROWS // 2, 2, 128), 'z', 0, 0, tiled...  43.6 us
    all_to_all x1, blocking collectives, per_device(): lax.all_to_all(send.reshape(64, 4, 128), ('yl', 'z'), 0, 0, tiled=True, a...  29.2 us
    all_to_all x1, blocking collectives, per_device(): got = lax.all_to_all(send, ('yh', 'yl', 'x'), 0, 0, tiled=True)  17.2 us
    ppermute x1, starting transfers between devices, per_device(): other = lax.ppermute(got, 'c', [(0, 1), (1, 0)])  4.75 us
    pallas_call x1, Pallas kernels, per_device(): pl.pallas_call(pack_kernel, out_shape=jax.ShapeDtypeStruct((SENDROWS * NZ...  2.6 us
  transfers between devices with their start and end apart: 1, of which 1 were waited for; matrix products, arithmetic and copies ran while one was open for 0% of the time, Pallas kernels for 1%

profile of v3, /device:TPU:1, one launch (start us, length us, event | category | flops | bytes accessed | tf_op | source)
XLA Modules:
  0.0 102.4 jit_solution(14323326634536339748)
XLA Ops:
  0.6 2.6 %pack.1 = bf16[320,128]{1,0:T(8,128)(2,1)} custom-call(bf16[224,64]{1,0:T(8,128)(2,1)} %bitcast.17, f32[224,64]{1,0:T(8,128)} %bitcast.12, bf16[448,64]{1,0:T(8,128)(2,1)} %bitcast.25, s32[1,56]{1,0:T(1,128)} %bitcast.19, s32[1,56]{1,0:T(1,128)} %bitcast.21), custom_call_target="tpu_custom_call" | custom-call | tf_op jit(solution)/shard_map/pack/pallas_call | solution.py:303
  3.2 43.6 %all_to_all.15 = bf16[160,2,128]{2,1,0:T(2,128)(2,1)S(1)} all-to-all(bf16[160,2,128]{2,1,0:T(2,128)(2,1)} %bitcast.24), channel_id=1, replica_groups={{160,168,176,184,192,200,208,216,224,232,240,248,0,8,16,24,32,40,48,56,..., dimensions={0} | all-to-all | bytes 163840 | tf_op jit(solution)/shard_map/to_planes/all_to_all | solution.py:319
  46.8 0.3 spread.1
  47.1 0.0 copy-start
  47.1 0.0 copy-start.1
  47.1 17.2 %all_to_all.16.after_hbm.own_ref = bf16[16,144,128]{2,1,0:T(8,128)(2,1)S(1)} all-to-all(bf16[16,144,128]{2,1,0:T(8,128)(2,1)S(1)} %spread.1), channel_id=1, replica_groups=mesh['yh'=2,'yl'=2,'z'=32,'x'=4,'c'=2] {'yh','yl','x'}, dimensions={0} | all-to-all | bytes 1179648 | tf_op jit(solution)/shard_map/in_plane/all_to_all | solution.py:329
  64.4 0.0 copy-start.2
  64.4 0.0 copy-start.3
  64.4 0.0 copy-start.4
  64.4 4.7 %collective-permute-start = (bf16[16,144,128]{2,1,0:T(8,128)(2,1)S(1)}, bf16[16,144,128]{2,1,0:T(8,128)(2,1)S(1)}, u32[]{:S(2)}, u32[]{:S(2)}) collective-permute-start(bf16[16,144,128]{2,1,0:T(8,128)(2,1)S(1)} %all_to_all.16.after_hbm.own_ref), channel_id=1, source_target_pairs={{0,1},{1,0},{2,3},{3,2},{4,5},{5,4},{6,7},{7,6},{8,9},{9,8},{10,11... | collective-permute-start | bytes 1769480 | tf_op jit(solution)/shard_map/cores/ppermute | solution.py:331
  69.1 0.0 copy-done
  69.1 0.0 copy-done.1
  69.1 0.0 copy-done.2
  69.1 0.0 copy-done.3
  69.2 0.0 copy-done.4
  69.2 1.1 %moment.1 = (f32[224,64]{1,0:T(8,128)}, s32[8,128]{1,0:T(8,128)S(1)}) custom-call(bf16[16,144,128]{2,1,0:T(8,128)(2,1)S(1)} %all_to_all.16.after_hbm.own_ref, bf16[224,64]{1,0:T(8,128)(2,1)S(1)} %bitcast.18, f32[224,64]{1,0:T(8,128)S(1)} %bitcast.13, s32[1,56]{1,0:T(1,128)S(1)} %bitcast.20, s32[1,56]{1,0:T(1,128)S(1)} %bitcast.23, s32[1,56]{1,0:T(1,128)S(1)} %bitcast.22), custom_call_target="tpu_custom_call" | custom-call | tf_op jit(solution)/shard_map/moment/pallas_call | solution.py:333
  70.2 0.5 collective-permute-done.other_ref
  70.7 1.6 %block.1 = bf16[256,128]{1,0:T(8,128)(2,1)S(1)} custom-call(bf16[16,144,128]{2,1,0:T(8,128)(2,1)S(1)} %all_to_all.16.after_hbm.own_ref, bf16[16,144,128]{2,1,0:T(8,128)(2,1)S(1)} %collective-permute-done.other_ref, s32[8,128]{1,0:T(8,128)S(1)} %get-tuple-element.7.table_hbm.table_ref), custom_call_target="tpu_custom_call" | custom-call | tf_op jit(solution)/shard_map/block/pallas_call | solution.py:352
  72.3 29.2 %all_to_all.17 = bf16[64,4,128]{2,1,0:T(4,128)(2,1)S(1)} all-to-all(bf16[64,4,128]{2,1,0:T(4,128)(2,1)S(1)} %bitcast.15), channel_id=1, replica_groups={{160,168,176,184,192,200,208,216,224,232,240,248,0,8,16,24,32,40,48,56,..., dimensions={0} | all-to-all | bytes 131072 | tf_op jit(solution)/shard_map/back/all_to_all | solution.py:361
  101.5 0.9 unpack.1
Async XLA Ops:
  47.1 22.0 %copy-start = (f32[56,4,64]{2,1,0:T(4,128)S(1)}, f32[56,4,64]{2,1,0:T(4,128)}, u32[]{:S(2)}) copy-start(f32[56,4,64]{2,1,0:T(4,128)} %param.7) | copy-start | bytes 172036
  47.1 22.0 %copy-start.1 = (bf16[56,4,64]{2,1,0:T(4,128)(2,1)S(1)}, bf16[56,4,64]{2,1,0:T(4,128)(2,1)}, u32[]{:S(2)}) copy-start(bf16[56,4,64]{2,1,0:T(4,128)(2,1)} %param.6) | copy-start | bytes 86020
  64.4 4.8 %copy-start.2 = (s32[56]{0:T(128)S(1)}, s32[56]{0:T(128)}, u32[]{:S(2)}) copy-start(s32[56]{0:T(128)} %param.9) | copy-start | bytes 676
  64.4 4.8 %copy-start.3 = (s32[56]{0:T(128)S(1)}, s32[56]{0:T(128)}, u32[]{:S(2)}) copy-start(s32[56]{0:T(128)} %param.11) | copy-start | bytes 676
  64.4 4.8 %copy-start.4 = (s32[56]{0:T(128)S(1)}, s32[56]{0:T(128)}, u32[]{:S(2)}) copy-start(s32[56]{0:T(128)} %param.10) | copy-start | bytes 676
  64.4 6.4 %collective-permute-start = (bf16[16,144,128]{2,1,0:T(8,128)(2,1)S(1)}, bf16[16,144,128]{2,1,0:T(8,128)(2,1)S(1)}, u32[]{:S(2)}, u32[]{:S(2)}) collective-permute-start(bf16[16,144,128]{2,1,0:T(8,128)(2,1)S(1)} %all_to_all.16.after_hbm.own_ref), channel_id=1, source_target_pairs={{0,1},{1,0},{2,3},{3,2},{4,5},{5,4},{6,7},{7,6},{8,9},{9,8},{10,11... | collective-permute-start | bytes 1769480 | tf_op jit(solution)/shard_map/cores/ppermute | solution.py:331

commit v4 on v3

--- a/solution.py
+++ b/solution.py
@@ -15,9 +15,12 @@
 NZ = 32
 SENDROWS = 10
 PLANE_FACTOR = 6554
-FIRST = 20
+FIRST = 22
+FIRST_BACK = 18
+LEAD = 10
+IN_PLANE = [[(k + LEAD) % 16 for k in range(16)]]
 ALONG_Z = [[(k + FIRST) % NZ for k in range(NZ)]]
-ALONG_YZ = [[y * NZ + (k + FIRST) % NZ for y in range(2) for k in range(NZ)]]
+ALONG_YZ = [[y * NZ + (k + FIRST_BACK) % NZ for y in range(2) for k in range(NZ)]]
 VMEM = pl.BlockSpec(memory_space=pltpu.VMEM)
 ANY = pl.BlockSpec(memory_space=pl.ANY)
 
@@ -81,12 +84,12 @@
     return wide, BETA_TWO * moment + (1.0 - BETA_TWO) * wide * wide
 
 
-def place(z):
-    return (z + (NZ - FIRST)) & (NZ - 1)
+def place(z, first):
+    return (z + (NZ - first)) & (NZ - 1)
 
 
 def seat_row(slot):
-    return ((slot & 1) * NZ + place(slot >> 1)) * 4
+    return ((slot & 1) * NZ + place(slot >> 1, FIRST_BACK)) * 4
 
 
 def dp_rank():
@@ -210,16 +213,16 @@
     n = SENDROWS * NZ
     got = in_ref[...]
     o, k = iota((256, n), 0), iota((256, n), 1)
-    pairs = pick(k == place((o >> 2) & 31) * SENDROWS + (o >> 7) * 4 + (o & 3), got).astype(BF16)
+    pairs = pick(k == place((o >> 2) & 31, FIRST) * SENDROWS + (o >> 7) * 4 + (o & 3), got).astype(BF16)
     o, k = iota((NZ, n), 0), iota((NZ, n), 1)
-    extra = pick(k == place(o) * SENDROWS + 8, got).astype(BF16)
+    extra = pick(k == place(o, FIRST) * SENDROWS + 8, got).astype(BF16)
     for e in range(2):
         lanes = slice(64 * e, 64 * e + 64)
         rest = jnp.concatenate([extra[:16, lanes], extra[16:, lanes]], axis=1)
         for dest in range(16):
             if (dest // 4) % 2 == e:
-                out_ref[dest, 0:128] = pairs[128 * e : 128 * e + 128]
-                out_ref[dest, 128:144] = rest
+                out_ref[(dest - LEAD) % 16, 0:128] = pairs[128 * e : 128 * e + 128]
+                out_ref[(dest - LEAD) % 16, 128:144] = rest
 
 
 def block_kernel(own_ref, other_ref, table_hbm, out_ref, mixed, grad, parts):
@@ -229,7 +232,7 @@
     def assemble(low_ref, high_ref):
         for yy in range(4):
             for xx in range(4):
-                i = yy * 4 + xx
+                i = (yy * 4 + xx - LEAD) % 16
                 rr, cc = slice(128 * yy, 128 * yy + 128), slice(128 * xx, 128 * xx + 128)
                 low, high = low_ref[i, 0:128, :], high_ref[i, 0:128, :]
                 mixed[rr, cc] = jnp.concatenate([low[:, :64], high[:, :64]], axis=1)
@@ -245,7 +248,11 @@
 
     extras = []
     for yy in range(4):
-        parts_of = [ref[4 * yy + xx, 128:144, :].astype(F32) for ref in (own_ref, other_ref) for xx in range(4)]
+        parts_of = [
+            ref[(4 * yy + xx - LEAD) % 16, 128:144, :].astype(F32)
+            for ref in (own_ref, other_ref)
+            for xx in range(4)
+        ]
         extras.append(sum(parts_of[1:], parts_of[0]))
     extra = jnp.concatenate(extras, axis=0)
     lane = iota((64, 128), 1) & 63
@@ -266,14 +273,17 @@
     shampoo = lax.dot_general(left, product, lanes, preferred_element_type=F32).astype(BF16)
     wide = shampoo.astype(F32)
     scale = jnp.sqrt(adam_sq / (whole_sum(wide * wide) + NORM_EPS))
-    direction = (scale * wide).astype(BF16)
+    direction = scale * wide
+    at = 4 * FIRST_BACK
     for hh in range(2):
+        ends = []
+        for row in (256 * hh, 256 * hh + 128):
+            ends += [direction[row + at : row + 128], direction[row : row + at]]
+        rows = jnp.concatenate(ends, axis=0).astype(BF16)
         for xx in range(4):
-            parts[4 * hh + xx] = direction[256 * hh : 256 * hh + 256, 128 * xx : 128 * xx + 128]
+            parts[4 * hh + xx] = rows[:, 128 * xx : 128 * xx + 128]
     mine = parts[4 * yh + x]
     mine = jnp.where(c == 0, mine[:, :64], mine[:, 64:])
-    at = 4 * FIRST
-    mine = jnp.concatenate([mine[at:128], mine[:at], mine[128 + at :], mine[128 : 128 + at]], axis=0)
     out_ref[...] = jnp.concatenate([mine, three_lanes(scale, iota((256, 64), 1)).astype(BF16)], axis=1)
 
 
@@ -291,6 +301,10 @@
         hit = iota((256, NB), 0) == table_ref[k + 1 : k + 2, 0:NB]
         grafts.append(whole_sum(jnp.where(hit, jnp.broadcast_to(scales, (256, NB)), 0.0)))
     graft_ref[...] = jnp.where(iota((1, 2), 1) == 0, grafts[0], grafts[1])
+
+
+def in_hbm(x):
+    return pltpu.with_memory_space_constraint(x, pltpu.HBM)
 
 
 def per_device(gradient, second_moment, factors, old_owner, new_owner, offsets):
@@ -313,8 +327,8 @@
                 index,
                 pltpu.SemaphoreType.DMA((5,)),
             ],
-            compiler_params=wide_params,
-        )(grad, moment, factors.reshape(8 * NB, 64), old, off)
+            compiler_params=params,
+        )(*(in_hbm(a) for a in (grad, moment, factors.reshape(8 * NB, 64), old, off)))
     with jax.named_scope("to_planes"):
         got = lax.all_to_all(send.reshape(NZ * SENDROWS // 2, 2, 128), "z", 0, 0, tiled=True, axis_index_groups=ALONG_Z)
     with jax.named_scope("spread"):
@@ -326,7 +340,7 @@
             compiler_params=params,
         )(got.reshape(SENDROWS * NZ, 128))
     with jax.named_scope("in_plane"):
-        got = lax.all_to_all(send, ("yh", "yl", "x"), 0, 0, tiled=True)
+        got = lax.all_to_all(send, ("yh", "yl", "x"), 0, 0, tiled=True, axis_index_groups=IN_PLANE)
     with jax.named_scope("cores"):
         other = lax.ppermute(got, "c", [(0, 1), (1, 0)])
     with jax.named_scope("moment"):

time: 103 us -> 98.4 us (0.955)
  blocking collectives: 90 us -> 87.4 us
  starting transfers between devices: 4.75 us -> 3.68 us
    all_to_all x1, blocking collectives: 17.2 us -> 15 us  [per_device(): lax.all_to_all(send, ('yh', 'yl', 'x'), 0, 0, tiled=True, axis_index_grou...]
    ppermute x1, starting transfers between devices: 4.75 us -> 3.68 us  [per_device(): other = lax.ppermute(got, 'c', [(0, 1), (1, 0)])]
where the time goes in v4:
time: 98.4 us; the launch traced here: 98.1 us
  blocking collectives  87.4 us (89%)
  Pallas kernels  5.78 us (6%)
  starting transfers between devices  3.68 us (4%)
    all_to_all x1, blocking collectives, per_device(): lax.all_to_all(send.reshape(NZ * SENDROWS // 2, 2, 128), 'z', 0, 0, tiled...  42.9 us
    all_to_all x1, blocking collectives, per_device(): lax.all_to_all(send.reshape(64, 4, 128), ('yl', 'z'), 0, 0, tiled=True, a...  29.5 us
    all_to_all x1, blocking collectives, per_device(): lax.all_to_all(send, ('yh', 'yl', 'x'), 0, 0, tiled=True, axis_index_grou...  15 us
    ppermute x1, starting transfers between devices, per_device(): other = lax.ppermute(got, 'c', [(0, 1), (1, 0)])  3.68 us
    pallas_call x1, Pallas kernels, per_device(): pl.pallas_call(pack_kernel, out_shape=jax.ShapeDtypeStruct((SENDROWS * NZ...  1.97 us
  transfers between devices with their start and end apart: 1, of which 1 were waited for; matrix products, arithmetic and copies ran while one was open for 0% of the time, Pallas kernels for 1%

profile of v4, /device:TPU:1, one launch (start us, length us, event | category | flops | bytes accessed | tf_op | source)
XLA Modules:
  0.0 98.1 jit_solution(4762307217419785208)
XLA Ops:
  0.6 2.0 %pack.1 = bf16[320,128]{1,0:T(8,128)(2,1)S(1)} custom-call(bf16[224,64]{1,0:T(8,128)(2,1)} %bitcast.18, f32[224,64]{1,0:T(8,128)} %bitcast.12, bf16[448,64]{1,0:T(8,128)(2,1)} %bitcast.25, s32[1,56]{1,0:T(1,128)} %bitcast.20, s32[1,56]{1,0:T(1,128)} %bitcast.22), custom_call_target="tpu_custom_call" | custom-call | tf_op jit(solution)/shard_map/pack/pallas_call | solution.py:317
  2.6 42.9 %all_to_all.15 = bf16[160,2,128]{2,1,0:T(2,128)(2,1)S(1)} all-to-all(bf16[160,2,128]{2,1,0:T(2,128)(2,1)S(1)} %bitcast.14), channel_id=1, replica_groups={{176,184,192,200,208,216,224,232,240,248,0,8,16,24,32,40,48,56,64,72,80..., dimensions={0} | all-to-all | bytes 163840 | tf_op jit(solution)/shard_map/to_planes/all_to_all | solution.py:333
  45.5 0.3 spread.1
  45.8 0.0 copy-start
  45.9 0.0 copy-start.1
  45.9 15.0 %all_to_all.16.after_hbm.own_ref = bf16[16,144,128]{2,1,0:T(8,128)(2,1)S(1)} all-to-all(bf16[16,144,128]{2,1,0:T(8,128)(2,1)S(1)} %spread.1), channel_id=1, replica_groups={{516,518,768,770,772,774,0,2,4,6,256,258,260,262,512,514},{517,519,769,..., dimensions={0} | all-to-all | bytes 1179648 | tf_op jit(solution)/shard_map/in_plane/all_to_all | solution.py:343
  60.9 0.0 copy-start.2
  60.9 0.0 copy-start.3
  60.9 0.0 copy-start.4
  60.9 3.7 %collective-permute-start = (bf16[16,144,128]{2,1,0:T(8,128)(2,1)S(1)}, bf16[16,144,128]{2,1,0:T(8,128)(2,1)S(1)}, u32[]{:S(2)}, u32[]{:S(2)}) collective-permute-start(bf16[16,144,128]{2,1,0:T(8,128)(2,1)S(1)} %all_to_all.16.after_hbm.own_ref), channel_id=1, source_target_pairs={{0,1},{1,0},{2,3},{3,2},{4,5},{5,4},{6,7},{7,6},{8,9},{9,8},{10,11... | collective-permute-start | bytes 1769480 | tf_op jit(solution)/shard_map/cores/ppermute | solution.py:345
  64.6 0.0 copy-done
  64.6 0.0 copy-done.1
  64.6 0.0 copy-done.2
  64.6 0.0 copy-done.3
  64.6 0.0 copy-done.4
  64.6 1.1 %moment.1 = (f32[224,64]{1,0:T(8,128)}, s32[8,128]{1,0:T(8,128)S(1)}) custom-call(bf16[16,144,128]{2,1,0:T(8,128)(2,1)S(1)} %all_to_all.16.after_hbm.own_ref, bf16[224,64]{1,0:T(8,128)(2,1)S(1)} %bitcast.19, f32[224,64]{1,0:T(8,128)S(1)} %bitcast.13, s32[1,56]{1,0:T(1,128)S(1)} %bitcast.21, s32[1,56]{1,0:T(1,128)S(1)} %bitcast.24, s32[1,56]{1,0:T(1,128)S(1)} %bitcast.23), custom_call_target="tpu_custom_call" | custom-call | tf_op jit(solution)/shard_map/moment/pallas_call | solution.py:347
  65.7 0.5 collective-permute-done.other_ref
  66.2 1.6 %block.1 = bf16[256,128]{1,0:T(8,128)(2,1)S(1)} custom-call(bf16[16,144,128]{2,1,0:T(8,128)(2,1)S(1)} %all_to_all.16.after_hbm.own_ref, bf16[16,144,128]{2,1,0:T(8,128)(2,1)S(1)} %collective-permute-done.other_ref, s32[8,128]{1,0:T(8,128)S(1)} %get-tuple-element.7.table_hbm.table_ref), custom_call_target="tpu_custom_call" | custom-call | tf_op jit(solution)/shard_map/block/pallas_call | solution.py:366
  67.8 29.5 %all_to_all.17 = bf16[64,4,128]{2,1,0:T(4,128)(2,1)S(1)} all-to-all(bf16[64,4,128]{2,1,0:T(4,128)(2,1)S(1)} %bitcast.16), channel_id=1, replica_groups={{144,152,160,168,176,184,192,200,208,216,224,232,240,248,0,8,16,24,32,4..., dimensions={0} | all-to-all | bytes 131072 | tf_op jit(solution)/shard_map/back/all_to_all | solution.py:375
  97.2 0.9 unpack.1
Async XLA Ops:
  45.8 18.7 %copy-start = (f32[56,4,64]{2,1,0:T(4,128)S(1)}, f32[56,4,64]{2,1,0:T(4,128)}, u32[]{:S(2)}) copy-start(f32[56,4,64]{2,1,0:T(4,128)} %param.7) | copy-start | bytes 172036
  45.9 18.7 %copy-start.1 = (bf16[56,4,64]{2,1,0:T(4,128)(2,1)S(1)}, bf16[56,4,64]{2,1,0:T(4,128)(2,1)}, u32[]{:S(2)}) copy-start(bf16[56,4,64]{2,1,0:T(4,128)(2,1)} %param.6) | copy-start | bytes 86020
  60.9 3.7 %copy-start.2 = (s32[56]{0:T(128)S(1)}, s32[56]{0:T(128)}, u32[]{:S(2)}) copy-start(s32[56]{0:T(128)} %param.9) | copy-start | bytes 676
  60.9 3.7 %copy-start.3 = (s32[56]{0:T(128)S(1)}, s32[56]{0:T(128)}, u32[]{:S(2)}) copy-start(s32[56]{0:T(128)} %param.11) | copy-start | bytes 676
  60.9 3.7 %copy-start.4 = (s32[56]{0:T(128)S(1)}, s32[56]{0:T(128)}, u32[]{:S(2)}) copy-start(s32[56]{0:T(128)} %param.10) | copy-start | bytes 676
  60.9 5.3 %collective-permute-start = (bf16[16,144,128]{2,1,0:T(8,128)(2,1)S(1)}, bf16[16,144,128]{2,1,0:T(8,128)(2,1)S(1)}, u32[]{:S(2)}, u32[]{:S(2)}) collective-permute-start(bf16[16,144,128]{2,1,0:T(8,128)(2,1)S(1)} %all_to_all.16.after_hbm.own_ref), channel_id=1, source_target_pairs={{0,1},{1,0},{2,3},{3,2},{4,5},{5,4},{6,7},{7,6},{8,9},{9,8},{10,11... | collective-permute-start | bytes 1769480 | tf_op jit(solution)/shard_map/cores/ppermute | solution.py:345

commit v5 on v4

--- a/solution.py
+++ b/solution.py
@@ -14,7 +14,6 @@
 NB = 56
 NZ = 32
 SENDROWS = 10
-PLANE_FACTOR = 6554
 FIRST = 22
 FIRST_BACK = 18
 LEAD = 10
@@ -105,7 +104,7 @@
 
 def pack_kernel(
     grad_hbm, moment_hbm, factor_hbm, old_hbm, off_hbm, send_ref,
-    grad_ref, moment_ref, factor_ref, old_ref, off_ref, sems,
+    grad_ref, moment_ref, factor_ref, old_ref, off_ref, stage, sems,
 ):
     copies = fetch(
         (
@@ -119,33 +118,26 @@
     )
     row0 = dp_rank() * 4
     col0 = (lax.axis_index("x") * 2 + lax.axis_index("c")) * 64
-    for copy in copies[:2]:
+    stage[...] = jnp.zeros((SENDROWS * NZ, 128), F32)
+    for copy in copies:
         copy.wait()
     old = old_ref[...]
     slot_col, off_col = to_column(slots_row(old, to_column(old))), to_column(off_ref[...])
     position = total(slot_col == iota((NB, NB), 1), jnp.broadcast_to(off_col, (NB, NB)), 0)
-    rows = SENDROWS * NZ
-    sent = iota((rows, NB), 0)
-    group = (sent * PLANE_FACTOR) >> 16
-    q = sent - SENDROWS * group
-    plane = (group + FIRST) & (NZ - 1)
-    seat = 2 * plane + ((q >> 2) & 1)
-    spread = total(iota((rows, NB), 1) == seat, jnp.broadcast_to(position, (rows, NB)), 1)
-    plane, q = plane[:, 0:1], q[:, 0:1]
-    r = q & 3
-    used = (q < 8) & (plane < NB // 2)
-    from_factor = jnp.where(used, (2 * plane + (q >> 2)) * 8 + r, -1)
-    from_grad = jnp.where(used, spread * 4 + r, jnp.where(q == 8, 4 * NB + plane, -9 * NB)) + 8 * NB
-    k = iota((rows, 12 * NB + NZ), 1)
-    mask = (k == from_factor) | (k == from_grad)
-    for copy in copies[2:]:
-        copy.wait()
+    rows = 4 * NB
+    spread = total(
+        iota((rows, NB), 1) == (iota((rows, NB), 0) >> 2),
+        jnp.broadcast_to(position, (rows, NB)),
+        1,
+    )
+    source = spread * 4 + (iota((rows, 1), 0) & 3)
     grad = grad_ref[...]
+    mine = pick(iota((rows, rows), 1) == source, grad)
     wide, moment = adam_moment(grad, moment_ref[...])
     step = wide / (jnp.sqrt(moment) + ADAM_EPS)
     by_row = jnp.sum(step * step, axis=1, keepdims=True)
-    mine = iota((4 * NB, NB), 1) == (iota((4 * NB, NB), 0) >> 2)
-    by_block = jnp.sum(jnp.where(mine, by_row, 0.0), axis=0, keepdims=True)
+    of_block = iota((rows, NB), 1) == (iota((rows, NB), 0) >> 2)
+    by_block = jnp.sum(jnp.where(of_block, by_row, 0.0), axis=0, keepdims=True)
     by_slot = jnp.sum(
         jnp.where(
             iota((NB, NB), 0) == jnp.broadcast_to(position, (NB, NB)), to_column_wide(by_block), 0.0
@@ -153,30 +145,31 @@
         axis=0,
         keepdims=True,
     )
-    factor = factor_ref[...].astype(F32)
-    r8, lane = iota((8 * NB, 64), 0) & 7, iota((8 * NB, 64), 1)
-    row, col = row0 + (r8 & 3), col0 + lane
-    right = pltpu.roll(factor, 8 * NB - 4, 0)
-    mixed = jnp.where(col > row, factor, right)
-    on_diagonal = jnp.sum(jnp.where((col == row) & (r8 < 4), factor, 0.0), axis=1, keepdims=True)
-    r8, lane = iota((8 * NB, 128), 0), iota((8 * NB, 128), 1)
-    seat_lane = 64 * ((r8 >> 3) & 1) + 8 + (r8 & 3)
-    on_diagonal = jnp.where(lane == seat_lane, on_diagonal, 0.0).astype(BF16)
-    extra = pick(iota((NZ, 8 * NB), 0) == (iota((NZ, 8 * NB), 1) >> 4), on_diagonal)
+    planes = NB // 2
+    factor = factor_ref[...].astype(F32).reshape(planes, 2, 8, 64)
+    first, second = factor[:, 0], factor[:, 1]
+    shape = (planes, 8, 64)
+    sub, lane = iota(shape, 1), iota(shape, 2)
+    row, col = row0 + (sub & 3), col0 + lane
+    left = jnp.where(sub < 4, first, pltpu.roll(second, 4, 1))
+    right = jnp.where(sub < 4, pltpu.roll(first, 4, 1), second)
+    mixed = jnp.where(col > row, left, right).reshape(rows, 64)
+    on_diagonal = jnp.sum(jnp.where(col == row, left, 0.0), axis=2, keepdims=True)
+    shape = (planes, 8, 128)
+    sub, lane = iota(shape, 1), iota(shape, 2)
+    seat_lane = 64 * (sub >> 2) + 8 + (sub & 3)
+    on_diagonal = jnp.sum(jnp.where(lane == seat_lane, on_diagonal, 0.0), axis=1, keepdims=True)
+    extra = jnp.zeros((NZ, 128), F32)
     p, s = iota((NZ, NB), 0), iota((NZ, NB), 1)
     for e in range(2):
         adam = jnp.sum(jnp.where(s == 2 * p + e, by_slot, 0.0), axis=1, keepdims=True)
         extra = extra + three_lanes(adam, iota((NZ, 128), 1) - 64 * e)
-    none = jnp.zeros((8 * NB, 64), BF16)
-    source = jnp.concatenate(
-        [
-            jnp.concatenate([mixed.astype(BF16), none], axis=1),
-            jnp.concatenate([none[: 4 * NB], grad], axis=1),
-            extra.astype(BF16),
-        ],
-        axis=0,
-    )
-    send_ref[...] = pick(mask, source).astype(BF16)
+    both = jnp.concatenate([mixed, mine], axis=1)
+    for plane in range(planes):
+        at = SENDROWS * ((plane - FIRST) % NZ)
+        stage[at : at + 8, :] = both[8 * plane : 8 * plane + 8]
+        stage[at + 8 : at + 9, :] = extra[plane : plane + 1] + on_diagonal[plane]
+    send_ref[...] = stage[...].astype(BF16)
 
 
 def moment_kernel(
@@ -273,17 +266,14 @@
     shampoo = lax.dot_general(left, product, lanes, preferred_element_type=F32).astype(BF16)
     wide = shampoo.astype(F32)
     scale = jnp.sqrt(adam_sq / (whole_sum(wide * wide) + NORM_EPS))
-    direction = scale * wide
+    for hh in range(2):
+        for xx in range(4):
+            parts[4 * hh + xx] = shampoo[256 * hh : 256 * hh + 256, 128 * xx : 128 * xx + 128]
+    mine = scale * parts[4 * yh + x].astype(F32)
+    mine = jnp.where(c == 0, mine[:, :64], mine[:, 64:])
     at = 4 * FIRST_BACK
-    for hh in range(2):
-        ends = []
-        for row in (256 * hh, 256 * hh + 128):
-            ends += [direction[row + at : row + 128], direction[row : row + at]]
-        rows = jnp.concatenate(ends, axis=0).astype(BF16)
-        for xx in range(4):
-            parts[4 * hh + xx] = rows[:, 128 * xx : 128 * xx + 128]
-    mine = parts[4 * yh + x]
-    mine = jnp.where(c == 0, mine[:, :64], mine[:, 64:])
+    mine = jnp.concatenate([mine[at:128], mine[:at], mine[128 + at :], mine[128 : 128 + at]], axis=0)
+    mine = mine.astype(BF16)
     out_ref[...] = jnp.concatenate([mine, three_lanes(scale, iota((256, 64), 1)).astype(BF16)], axis=1)
 
 
@@ -311,7 +301,6 @@
     old, own, off = (a.reshape(1, NB) for a in (old_owner, new_owner, offsets))
     grad, moment = gradient.reshape(4 * NB, 64), second_moment.reshape(4 * NB, 64)
     params = pltpu.CompilerParams(vmem_limit_bytes=40 * 1024 * 1024)
-    wide_params = pltpu.CompilerParams(vmem_limit_bytes=60 * 1024 * 1024)
     index = pltpu.VMEM((1, NB), jnp.int32)
     with jax.named_scope("pack"):
         send = pl.pallas_call(
@@ -325,6 +314,7 @@
                 pltpu.VMEM((8 * NB, 64), BF16),
                 index,
                 index,
+                pltpu.VMEM((SENDROWS * NZ, 128), F32),
                 pltpu.SemaphoreType.DMA((5,)),
             ],
             compiler_params=params,

time: 98.4 us -> 98 us (level)
  no operation moved by 1% of the time
where the time goes in v5:
time: 98 us; the launch traced here: 97.7 us
  blocking collectives  87.4 us (89%)
  Pallas kernels  5.34 us (5%)
  starting transfers between devices  3.68 us (4%)
    all_to_all x1, blocking collectives, per_device(): lax.all_to_all(send.reshape(NZ * SENDROWS // 2, 2, 128), 'z', 0, 0, tiled...  42.9 us
    all_to_all x1, blocking collectives, per_device(): lax.all_to_all(send.reshape(64, 4, 128), ('yl', 'z'), 0, 0, tiled=True, a...  29.5 us
    all_to_all x1, blocking collectives, per_device(): lax.all_to_all(send, ('yh', 'yl', 'x'), 0, 0, tiled=True, axis_index_grou...  15 us
    ppermute x1, starting transfers between devices, per_device(): other = lax.ppermute(got, 'c', [(0, 1), (1, 0)])  3.68 us
  transfers between devices with their start and end apart: 1, of which 1 were waited for; matrix products, arithmetic and copies ran while one was open for 0% of the time, Pallas kernels for 1%

profile of v5, /device:TPU:1, one launch (start us, length us, event | category | flops | bytes accessed | tf_op | source)
XLA Modules:
  0.0 97.7 jit_solution(15503099864247790663)
XLA Ops:
  0.6 1.7 %pack.1 = bf16[320,128]{1,0:T(8,128)(2,1)S(1)} custom-call(bf16[224,64]{1,0:T(8,128)(2,1)} %bitcast.18, f32[224,64]{1,0:T(8,128)} %bitcast.12, bf16[448,64]{1,0:T(8,128)(2,1)} %bitcast.25, s32[1,56]{1,0:T(1,128)} %bitcast.20, s32[1,56]{1,0:T(1,128)} %bitcast.22), custom_call_target="tpu_custom_call" | custom-call | tf_op jit(solution)/shard_map/pack/pallas_call | solution.py:306
  2.3 42.9 %all_to_all.15 = bf16[160,2,128]{2,1,0:T(2,128)(2,1)S(1)} all-to-all(bf16[160,2,128]{2,1,0:T(2,128)(2,1)S(1)} %bitcast.14), channel_id=1, replica_groups={{176,184,192,200,208,216,224,232,240,248,0,8,16,24,32,40,48,56,64,72,80..., dimensions={0} | all-to-all | bytes 163840 | tf_op jit(solution)/shard_map/to_planes/all_to_all | solution.py:323
  45.2 0.3 spread.1
  45.5 0.0 copy-start
  45.5 0.0 copy-start.1
  45.6 15.0 %all_to_all.16.after_hbm.own_ref = bf16[16,144,128]{2,1,0:T(8,128)(2,1)S(1)} all-to-all(bf16[16,144,128]{2,1,0:T(8,128)(2,1)S(1)} %spread.1), channel_id=1, replica_groups={{516,518,768,770,772,774,0,2,4,6,256,258,260,262,512,514},{517,519,769,..., dimensions={0} | all-to-all | bytes 1179648 | tf_op jit(solution)/shard_map/in_plane/all_to_all | solution.py:333
  60.6 0.0 copy-start.2
  60.6 0.0 copy-start.3
  60.6 0.0 copy-start.4
  60.6 3.7 %collective-permute-start = (bf16[16,144,128]{2,1,0:T(8,128)(2,1)S(1)}, bf16[16,144,128]{2,1,0:T(8,128)(2,1)S(1)}, u32[]{:S(2)}, u32[]{:S(2)}) collective-permute-start(bf16[16,144,128]{2,1,0:T(8,128)(2,1)S(1)} %all_to_all.16.after_hbm.own_ref), channel_id=1, source_target_pairs={{0,1},{1,0},{2,3},{3,2},{4,5},{5,4},{6,7},{7,6},{8,9},{9,8},{10,11... | collective-permute-start | bytes 1769480 | tf_op jit(solution)/shard_map/cores/ppermute | solution.py:335
  64.3 0.0 copy-done
  64.3 0.0 copy-done.1
  64.3 0.0 copy-done.2
  64.3 0.0 copy-done.3
  64.3 0.0 copy-done.4
  64.3 1.1 %moment.1 = (f32[224,64]{1,0:T(8,128)}, s32[8,128]{1,0:T(8,128)S(1)}) custom-call(bf16[16,144,128]{2,1,0:T(8,128)(2,1)S(1)} %all_to_all.16.after_hbm.own_ref, bf16[224,64]{1,0:T(8,128)(2,1)S(1)} %bitcast.19, f32[224,64]{1,0:T(8,128)S(1)} %bitcast.13, s32[1,56]{1,0:T(1,128)S(1)} %bitcast.21, s32[1,56]{1,0:T(1,128)S(1)} %bitcast.24, s32[1,56]{1,0:T(1,128)S(1)} %bitcast.23), custom_call_target="tpu_custom_call" | custom-call | tf_op jit(solution)/shard_map/moment/pallas_call | solution.py:337
  65.4 0.5 collective-permute-done.other_ref
  65.9 1.4 %block.1 = bf16[256,128]{1,0:T(8,128)(2,1)S(1)} custom-call(bf16[16,144,128]{2,1,0:T(8,128)(2,1)S(1)} %all_to_all.16.after_hbm.own_ref, bf16[16,144,128]{2,1,0:T(8,128)(2,1)S(1)} %collective-permute-done.other_ref, s32[8,128]{1,0:T(8,128)S(1)} %get-tuple-element.7.table_hbm.table_ref), custom_call_target="tpu_custom_call" | custom-call | tf_op jit(solution)/shard_map/block/pallas_call | solution.py:356
  67.3 29.5 %all_to_all.17 = bf16[64,4,128]{2,1,0:T(4,128)(2,1)S(1)} all-to-all(bf16[64,4,128]{2,1,0:T(4,128)(2,1)S(1)} %bitcast.16), channel_id=1, replica_groups={{144,152,160,168,176,184,192,200,208,216,224,232,240,248,0,8,16,24,32,4..., dimensions={0} | all-to-all | bytes 131072 | tf_op jit(solution)/shard_map/back/all_to_all | solution.py:365
  96.8 0.9 unpack.1
Async XLA Ops:
  45.5 18.7 %copy-start = (f32[56,4,64]{2,1,0:T(4,128)S(1)}, f32[56,4,64]{2,1,0:T(4,128)}, u32[]{:S(2)}) copy-start(f32[56,4,64]{2,1,0:T(4,128)} %param.7) | copy-start | bytes 172036
  45.5 18.7 %copy-start.1 = (bf16[56,4,64]{2,1,0:T(4,128)(2,1)S(1)}, bf16[56,4,64]{2,1,0:T(4,128)(2,1)}, u32[]{:S(2)}) copy-start(bf16[56,4,64]{2,1,0:T(4,128)(2,1)} %param.6) | copy-start | bytes 86020
  60.6 3.7 %copy-start.2 = (s32[56]{0:T(128)S(1)}, s32[56]{0:T(128)}, u32[]{:S(2)}) copy-start(s32[56]{0:T(128)} %param.9) | copy-start | bytes 676
  60.6 3.7 %copy-start.3 = (s32[56]{0:T(128)S(1)}, s32[56]{0:T(128)}, u32[]{:S(2)}) copy-start(s32[56]{0:T(128)} %param.11) | copy-start | bytes 676
  60.6 3.7 %copy-start.4 = (s32[56]{0:T(128)S(1)}, s32[56]{0:T(128)}, u32[]{:S(2)}) copy-start(s32[56]{0:T(128)} %param.10) | copy-start | bytes 676
  60.6 5.3 %collective-permute-start = (bf16[16,144,128]{2,1,0:T(8,128)(2,1)S(1)}, bf16[16,144,128]{2,1,0:T(8,128)(2,1)S(1)}, u32[]{:S(2)}, u32[]{:S(2)}) collective-permute-start(bf16[16,144,128]{2,1,0:T(8,128)(2,1)S(1)} %all_to_all.16.after_hbm.own_ref), channel_id=1, source_target_pairs={{0,1},{1,0},{2,3},{3,2},{4,5},{5,4},{6,7},{7,6},{8,9},{9,8},{10,11... | collective-permute-start | bytes 1769480 | tf_op jit(solution)/shard_map/cores/ppermute | solution.py:335
